TPU v7x, 32 devices: a whole 2x2x4 slice. The times are simulated.
32 devices in a mesh: seq: 4 (over y, x), dp: 8 (over z, core).
Axes of the slice: x: 2, y: 2, z: 4, core: 2. Of those that a mesh axis runs over, the one named last changes fastest.
Arguments:
- tokens: bfloat16 [8, 4, 784, 512], P('dp', 'seq'), may hold values from -6 to 6
- cotangent: bfloat16 [8, 4, 784, 512], P('dp', 'seq'), may hold values from -6 to 6
- norm1_gain: bfloat16 [512], P('dp'), may hold values from 0.25 to 1.75
- norm1_bias: bfloat16 [512], P('dp'), may hold values from -1.75 to 1.75
- qkv_weight: bfloat16 [512, 1536], P('dp'), may hold values from -0.25 to 0.25
- query_bias: bfloat16 [512], P('dp'), may hold values from -1.75 to 1.75
- value_bias: bfloat16 [512], P('dp'), may hold values from -1.75 to 1.75
- proj_weight: bfloat16 [512, 512], P('dp'), may hold values from -1 to 1
- proj_bias: bfloat16 [512], P('dp'), may hold values from -1.75 to 1.75
- norm2_gain: bfloat16 [512], P('dp'), may hold values from 0.25 to 1.75
- norm2_bias: bfloat16 [512], P('dp'), may hold values from -1.75 to 1.75
- fc1_weight: bfloat16 [512, 2048], P('dp'), may hold values from -0.25 to 0.25
- fc1_bias: bfloat16 [2048], P('dp'), may hold values from -1.75 to 1.75
- fc2_weight: bfloat16 [2048, 512], P('dp'), may hold values from -0.125 to 0.125
- fc2_bias: bfloat16 [512], P('dp'), may hold values from -1.75 to 1.75
- bias_table: float32 [169, 16], replicated, may hold values from -6 to 6
- region_ids: int32 [56, 56], replicated, may hold values from 0 to 8, as said below
- rel_index: int32 [49, 49], replicated, may hold values from 0 to 168, as said below
Outputs:
- output: bfloat16 [8, 4, 784, 512], P('dp', 'seq')
- input_grad: bfloat16 [8, 4, 784, 512], P('dp', 'seq')
- grad_norm1_gain: float32 [512], P('dp')
- grad_norm1_bias: float32 [512], P('dp')
- grad_qkv_weight: float32 [512, 1536], P('dp')
- grad_query_bias: float32 [512], P('dp')
- grad_value_bias: float32 [512], P('dp')
- grad_proj_weight: float32 [512, 512], P('dp')
- grad_proj_bias: float32 [512], P('dp')
- grad_norm2_gain: float32 [512], P('dp')
- grad_norm2_bias: float32 [512], P('dp')
- grad_fc1_weight: float32 [512, 2048], P('dp')
- grad_fc1_bias: float32 [2048], P('dp')
- grad_fc2_weight: float32 [2048, 512], P('dp')
- grad_fc2_bias: float32 [512], P('dp')
- grad_bias_table: float32 [169, 16], replicated
Inputs may be any that keep to these rules, and one draw needn't show every extreme that they name: region_ids[i, j] = 3 a_i + b_j, where each row i has its own a_i and each column j its own b_j, both 0, 1 or 2; all nine values occur. rel_index[a, b] depends only on the offset between positions a and b of the 7 x 7 window (row-major); different offsets give different rows, and every row of the table is used.
All inputs are finite; a program needn't handle non-finite values.
Results may differ from a plain program's by a relative error of at most 0.019.
Values may be sent and summed in bfloat16 or wider, within the bound.
A program may use at most 128 MiB of HBM per device.

v0:
```python
import jax
import jax.numpy as jnp
from jax import lax
from jax.sharding import PartitionSpec as P

HIGHEST = lax.Precision.HIGHEST


def partner(block, axis, distance):
    count = lax.axis_size(axis)
    route = []
    for low in range(count):
        high = low | 1 << distance
        if high != low and high < count:
            route += [(low, high), (high, low)]
    return lax.ppermute(block, axis, route)


def shifted_2(value, axis, steps):
    count = lax.axis_size(axis)
    pairs = [(source, (source + steps) % count) for source in range(count)]
    return lax.ppermute(value, axis, pairs)


def normalize(values, gain, shift):
    center = values - jnp.mean(values, -1, keepdims=True)
    scaled = lax.rsqrt(jnp.mean(center * center, -1, keepdims=True) + 1e-05)
    unit = center * scaled
    return (unit * gain + shift, unit, scaled)


def normalize_back(grad, unit, scaled, gain):
    inner = grad * gain
    return scaled * (
        inner
        - jnp.mean(inner, -1, keepdims=True)
        - unit * jnp.mean(inner * unit, -1, keepdims=True)
    )


def to_windows(field):
    batch, rows, cols, width = field.shape
    return (
        field.reshape(batch, rows // 7, 7, cols // 7, 7, width)
        .transpose(0, 1, 3, 2, 4, 5)
        .reshape(-1, 49, width)
    )


def from_windows(blocks, batch, rows, cols):
    width = blocks.shape[-1]
    return (
        blocks.reshape(batch, rows // 7, cols // 7, 7, 7, width)
        .transpose(0, 1, 3, 2, 4, 5)
        .reshape(batch, rows, cols, width)
    )


def roll_ahead(field):
    below = partner(field[:, :3], "seq", 0)
    field = jnp.concatenate([field[:, 3:], below], 1)
    beside = shifted_2(field[:, :, :3], "seq", -2)
    return jnp.concatenate([field[:, :, 3:], beside], 2)


def roll_behind(field):
    above = partner(field[:, -3:], "seq", 0)
    field = jnp.concatenate([above, field[:, :-3]], 1)
    beside = shifted_2(field[:, :, -3:], "seq", 2)
    return jnp.concatenate([beside, field[:, :, :-3]], 2)


def matmul_plain(left, right):
    return jnp.dot(left, right, preferred_element_type=jnp.float32)


def left_inner(left, right):
    return lax.dot_general(
        left, right, (((0,), (0,)), ((), ())), preferred_element_type=jnp.float32
    )


def right_inner(left, right):
    return lax.dot_general(
        left, right, (((1,), (1,)), ((), ())), preferred_element_type=jnp.float32
    )


def logits_of(queries, keys, extra, scale):
    return (
        jnp.einsum("wqhe,wkhe->whqk", queries, keys, preferred_element_type=jnp.float32) * scale
        + extra
    )


def local(
    tokens,
    cotangent,
    norm1_gain,
    norm1_bias,
    qkv_weight,
    query_bias,
    value_bias,
    proj_weight,
    proj_bias,
    norm2_gain,
    norm2_bias,
    fc1_weight,
    fc1_bias,
    fc2_weight,
    fc2_bias,
    bias_table,
    region_ids,
    rel_index,
):
    batch = tokens.shape[0]
    dim = tokens.shape[-1]
    heads = bias_table.shape[1]
    width = dim // heads
    scale = width ** (-0.5)
    image_rows, image_cols = region_ids.shape
    seq_count = lax.axis_size("seq")
    tile_rows = image_rows // 2
    tile_cols = image_cols * 2 // seq_count
    place = lax.axis_index("seq")
    regions = lax.dynamic_slice(
        region_ids, (place % 2 * tile_rows, place // 2 * tile_cols), (tile_rows, tile_cols)
    )
    region_win = to_windows(regions[None, :, :, None])[:, :, 0]
    mask = jnp.where(region_win[:, :, None] == region_win[:, None, :], 0.0, -100.0).astype(
        jnp.float32
    )
    mask = jnp.tile(mask, (batch, 1, 1))
    onehot = (
        rel_index.reshape(-1)[:, None] == jnp.arange(bias_table.shape[0], dtype=jnp.int32)[None, :]
    ).astype(jnp.float32)
    bias = jnp.dot(onehot, bias_table, precision=HIGHEST).reshape(49, 49, heads).transpose(2, 0, 1)
    extra = bias[None] + mask[:, None]
    gathered = (
        lax.all_gather(norm1_gain, "dp", axis=0, tiled=True),
        lax.all_gather(norm1_bias, "dp", axis=0, tiled=True),
        lax.all_gather(qkv_weight, "dp", axis=0, tiled=True),
        lax.all_gather(query_bias, "dp", axis=0, tiled=True),
        lax.all_gather(value_bias, "dp", axis=0, tiled=True),
        lax.all_gather(proj_weight, "dp", axis=0, tiled=True),
        lax.all_gather(proj_bias, "dp", axis=0, tiled=True),
        lax.all_gather(norm2_gain, "dp", axis=0, tiled=True),
        lax.all_gather(norm2_bias, "dp", axis=0, tiled=True),
        lax.all_gather(fc1_weight, "dp", axis=0, tiled=True),
        lax.all_gather(fc1_bias, "dp", axis=0, tiled=True),
        lax.all_gather(fc2_weight, "dp", axis=0, tiled=True),
        lax.all_gather(fc2_bias, "dp", axis=0, tiled=True),
    )
    (
        gain_one,
        shift_one,
        qkv_full,
        qbias_full,
        vbias_full,
        proj_full,
        pbias_full,
        gain_two,
        shift_two,
        fc1_full,
        fc1b_full,
        fc2_full,
        fc2b_full,
    ) = gathered
    gain_one = gain_one.astype(jnp.float32)
    gain_two = gain_two.astype(jnp.float32)
    source = tokens.reshape(batch, tile_rows, tile_cols, dim).astype(jnp.float32)
    first_norm, unit_one, scaled_one = normalize(source, gain_one, shift_one.astype(jnp.float32))
    shifted = roll_ahead(first_norm.astype(jnp.bfloat16))
    flat = to_windows(shifted).reshape(-1, dim)
    qkv_bias = jnp.concatenate(
        [
            qbias_full.astype(jnp.float32),
            jnp.zeros((dim,), jnp.float32),
            vbias_full.astype(jnp.float32),
        ]
    )
    projected = matmul_plain(flat, qkv_full) + qkv_bias
    queries = projected[:, :dim].astype(jnp.bfloat16).reshape(-1, 49, heads, width)
    keys = projected[:, dim : 2 * dim].astype(jnp.bfloat16).reshape(-1, 49, heads, width)
    values = projected[:, 2 * dim :].astype(jnp.bfloat16).reshape(-1, 49, heads, width)
    scores = logits_of(queries, keys, extra, scale)
    highest = jnp.max(scores, -1, keepdims=True)
    log_total = highest + jnp.log(jnp.sum(jnp.exp(scores - highest), -1, keepdims=True))
    probs = jnp.exp(scores - log_total).astype(jnp.bfloat16)
    mixed = jnp.einsum("whqk,wkhe->wqhe", probs, values, preferred_element_type=jnp.float32).astype(
        jnp.bfloat16
    )
    restored = roll_behind(
        from_windows(mixed.reshape(-1, 49, dim), batch, tile_rows, tile_cols)
    ).reshape(-1, dim)
    resid = (
        source.reshape(-1, dim) + matmul_plain(restored, proj_full) + pbias_full.astype(jnp.float32)
    )
    second_norm, unit_two, scaled_two = normalize(resid, gain_two, shift_two.astype(jnp.float32))
    second = second_norm.astype(jnp.bfloat16)
    before = matmul_plain(second, fc1_full) + fc1b_full.astype(jnp.float32)
    hidden = jax.nn.gelu(before, approximate=False).astype(jnp.bfloat16)
    output = (resid + matmul_plain(hidden, fc2_full) + fc2b_full.astype(jnp.float32)).astype(
        jnp.bfloat16
    )
    regathered = (
        lax.all_gather(norm1_gain, "dp", axis=0, tiled=True),
        lax.all_gather(norm1_bias, "dp", axis=0, tiled=True),
        lax.all_gather(qkv_weight, "dp", axis=0, tiled=True),
        lax.all_gather(query_bias, "dp", axis=0, tiled=True),
        lax.all_gather(value_bias, "dp", axis=0, tiled=True),
        lax.all_gather(proj_weight, "dp", axis=0, tiled=True),
        lax.all_gather(proj_bias, "dp", axis=0, tiled=True),
        lax.all_gather(norm2_gain, "dp", axis=0, tiled=True),
        lax.all_gather(norm2_bias, "dp", axis=0, tiled=True),
        lax.all_gather(fc1_weight, "dp", axis=0, tiled=True),
        lax.all_gather(fc1_bias, "dp", axis=0, tiled=True),
        lax.all_gather(fc2_weight, "dp", axis=0, tiled=True),
        lax.all_gather(fc2_bias, "dp", axis=0, tiled=True),
    )
    qkv_full = regathered[2]
    proj_full = regathered[5]
    fc1_full = regathered[9]
    fc2_full = regathered[11]
    grad_out = cotangent.reshape(-1, dim)
    grad_fc2 = left_inner(hidden, grad_out)
    grad_fc2b = jnp.sum(grad_out.astype(jnp.float32), 0)
    grad_hidden = right_inner(grad_out, fc2_full)
    normal_cdf = 0.5 * (1.0 + lax.erf(before * 0.7071067811865476))
    normal_pdf = jnp.exp(-0.5 * before * before) * 0.3989422804014327
    grad_before = (grad_hidden * (normal_cdf + before * normal_pdf)).astype(jnp.bfloat16)
    grad_fc1 = left_inner(second, grad_before)
    grad_fc1b = jnp.sum(grad_before.astype(jnp.float32), 0)
    grad_second = right_inner(grad_before, fc1_full)
    grad_gain2 = jnp.sum(grad_second * unit_two, 0)
    grad_shift2 = jnp.sum(grad_second, 0)
    grad_resid = grad_out.astype(jnp.float32) + normalize_back(
        grad_second, unit_two, scaled_two, gain_two
    )
    grad_pbias = jnp.sum(grad_resid, 0)
    grad_branch = grad_resid.astype(jnp.bfloat16)
    grad_proj = left_inner(restored, grad_branch)
    grad_restored = (
        right_inner(grad_branch, proj_full)
        .astype(jnp.bfloat16)
        .reshape(batch, tile_rows, tile_cols, dim)
    )
    grad_mixed = to_windows(roll_ahead(grad_restored)).reshape(-1, 49, heads, width)
    probs_full = jnp.exp(logits_of(queries, keys, extra, scale) - log_total)
    probs_low = probs_full.astype(jnp.bfloat16)
    grad_probs = jnp.einsum(
        "wqhe,wkhe->whqk", grad_mixed, values, preferred_element_type=jnp.float32
    )
    grad_values = jnp.einsum(
        "whqk,wqhe->wkhe", probs_low, grad_mixed, preferred_element_type=jnp.float32
    ).astype(jnp.bfloat16)
    grad_scores = (
        probs_full * (grad_probs - jnp.sum(grad_probs * probs_full, -1, keepdims=True))
    ).astype(jnp.bfloat16)
    grad_queries = (
        jnp.einsum("whqk,wkhe->wqhe", grad_scores, keys, preferred_element_type=jnp.float32) * scale
    ).astype(jnp.bfloat16)
    grad_keys = (
        jnp.einsum("whqk,wqhe->wkhe", grad_scores, queries, preferred_element_type=jnp.float32)
        * scale
    ).astype(jnp.bfloat16)
    score_sum = jnp.sum(grad_scores.astype(jnp.float32), 0)
    grad_table = jnp.dot(
        onehot.T, score_sum.transpose(1, 2, 0).reshape(-1, heads), precision=HIGHEST
    )
    grad_qkv_rows = jnp.concatenate(
        [grad_queries.reshape(-1, dim), grad_keys.reshape(-1, dim), grad_values.reshape(-1, dim)], 1
    )
    grad_qkv = left_inner(flat, grad_qkv_rows)
    grad_qbias = jnp.sum(grad_queries.reshape(-1, dim).astype(jnp.float32), 0)
    grad_vbias = jnp.sum(grad_values.reshape(-1, dim).astype(jnp.float32), 0)
    grad_flat = right_inner(grad_qkv_rows, qkv_full).astype(jnp.bfloat16)
    grad_first = roll_behind(
        from_windows(grad_flat.reshape(-1, 49, dim), batch, tile_rows, tile_cols)
    ).astype(jnp.float32)
    grad_gain1 = jnp.sum((grad_first * unit_one).reshape(-1, dim), 0)
    grad_shift1 = jnp.sum(grad_first.reshape(-1, dim), 0)
    grad_source = (
        normalize_back(grad_first, unit_one, scaled_one, gain_one).reshape(-1, dim) + grad_resid
    )
    input_grad = grad_source.astype(jnp.bfloat16).reshape(tokens.shape)
    owned = (
        lax.psum_scatter(
            grad_gain1.astype(jnp.bfloat16), "dp", scatter_dimension=0, tiled=True
        ).astype(jnp.float32),
        lax.psum_scatter(
            grad_shift1.astype(jnp.bfloat16), "dp", scatter_dimension=0, tiled=True
        ).astype(jnp.float32),
        lax.psum_scatter(
            grad_qkv.astype(jnp.bfloat16), "dp", scatter_dimension=0, tiled=True
        ).astype(jnp.float32),
        lax.psum_scatter(
            grad_qbias.astype(jnp.bfloat16), "dp", scatter_dimension=0, tiled=True
        ).astype(jnp.float32),
        lax.psum_scatter(
            grad_vbias.astype(jnp.bfloat16), "dp", scatter_dimension=0, tiled=True
        ).astype(jnp.float32),
        lax.psum_scatter(
            grad_proj.astype(jnp.bfloat16), "dp", scatter_dimension=0, tiled=True
        ).astype(jnp.float32),
        lax.psum_scatter(
            grad_pbias.astype(jnp.bfloat16), "dp", scatter_dimension=0, tiled=True
        ).astype(jnp.float32),
        lax.psum_scatter(
            grad_gain2.astype(jnp.bfloat16), "dp", scatter_dimension=0, tiled=True
        ).astype(jnp.float32),
        lax.psum_scatter(
            grad_shift2.astype(jnp.bfloat16), "dp", scatter_dimension=0, tiled=True
        ).astype(jnp.float32),
        lax.psum_scatter(
            grad_fc1.astype(jnp.bfloat16), "dp", scatter_dimension=0, tiled=True
        ).astype(jnp.float32),
        lax.psum_scatter(
            grad_fc1b.astype(jnp.bfloat16), "dp", scatter_dimension=0, tiled=True
        ).astype(jnp.float32),
        lax.psum_scatter(
            grad_fc2.astype(jnp.bfloat16), "dp", scatter_dimension=0, tiled=True
        ).astype(jnp.float32),
        lax.psum_scatter(
            grad_fc2b.astype(jnp.bfloat16), "dp", scatter_dimension=0, tiled=True
        ).astype(jnp.float32),
    )
    shards = (
        lax.psum(owned[0].astype(jnp.bfloat16), "seq").astype(jnp.float32),
        lax.psum(owned[1].astype(jnp.bfloat16), "seq").astype(jnp.float32),
        lax.psum(owned[2].astype(jnp.bfloat16), "seq").astype(jnp.float32),
        lax.psum(owned[3].astype(jnp.bfloat16), "seq").astype(jnp.float32),
        lax.psum(owned[4].astype(jnp.bfloat16), "seq").astype(jnp.float32),
        lax.psum(owned[5].astype(jnp.bfloat16), "seq").astype(jnp.float32),
        lax.psum(owned[6].astype(jnp.bfloat16), "seq").astype(jnp.float32),
        lax.psum(owned[7].astype(jnp.bfloat16), "seq").astype(jnp.float32),
        lax.psum(owned[8].astype(jnp.bfloat16), "seq").astype(jnp.float32),
        lax.psum(owned[9].astype(jnp.bfloat16), "seq").astype(jnp.float32),
        lax.psum(owned[10].astype(jnp.bfloat16), "seq").astype(jnp.float32),
        lax.psum(owned[11].astype(jnp.bfloat16), "seq").astype(jnp.float32),
        lax.psum(owned[12].astype(jnp.bfloat16), "seq").astype(jnp.float32),
    )
    table_total = lax.psum(grad_table, ("seq", "dp"))
    return (
        output.reshape(tokens.shape),
        input_grad,
        shards[0],
        shards[1],
        shards[2],
        shards[3],
        shards[4],
        shards[5],
        shards[6],
        shards[7],
        shards[8],
        shards[9],
        shards[10],
        shards[11],
        shards[12],
        table_total,
    )


def solution(mesh):
    in_specs = (
        P("dp", "seq", None, None),
        P("dp", "seq", None, None),
        P("dp"),
        P("dp"),
        P("dp", None),
        P("dp"),
        P("dp"),
        P("dp", None),
        P("dp"),
        P("dp"),
        P("dp"),
        P("dp", None),
        P("dp"),
        P("dp", None),
        P("dp"),
        P(),
        P(),
        P(),
    )
    out_specs = (
        P("dp", "seq", None, None),
        P("dp", "seq", None, None),
        P("dp"),
        P("dp"),
        P("dp", None),
        P("dp"),
        P("dp"),
        P("dp", None),
        P("dp"),
        P("dp"),
        P("dp"),
        P("dp", None),
        P("dp"),
        P("dp", None),
        P("dp"),
        P(),
    )
    return jax.shard_map(local, mesh=mesh, in_specs=in_specs, out_specs=out_specs, check_vma=False)
```

profile of v0, /device:TPU:0, one launch (start us, length us, event | category | flops | bytes accessed | tf_op | source)
XLA Modules:
  0.0 421.3 jit_solution(6543661096463967100)
XLA Ops:
  15.9 19.5 %all-reduce.18 = (bf16[512]{0:T(512)(128)(2,1)S(1)}, bf16[512]{0:T(512)(128)(2,1)S(1)}, bf16[512]{0:T(512)(128)(2,1)S(1)}, bf16[512]{0:T(512)(128)(2,1)S(1)}, bf...) all-reduce(bf16[512]{0:T(512)(128)(2,1)S(1)} %dynamic-update-slice., ...), channel_id=1, replica_groups=mesh['seq'=4,'dp'=8] {'dp'}, use_global_device_ids=true, to_apply=%add.1 | all-reduce | flops 3584 | bytes 14336
  59.1 4.1 maximum_reduce_fusion
  71.9 4.4 %copy.81 = bf16[16,49,16,32]{1,3,2,0:T(8,128)(2,1)S(1)} copy(bf16[16,49,16,32]{3,2,1,0:T(8,128)(2,1)} %reshape.456) | data formatting | bytes 1605632 | tf_op jit(solution)/shard_map/reshape | solution.py:184
  76.3 4.9 %reshape.455 = bf16[16,49,16,32]{3,2,1,0:T(8,128)(2,1)} reshape(bf16[784,512]{1,0:T(8,128)(2,1)} %get-tuple-element.62) | data formatting | bytes 1605632 | tf_op jit(solution)/shard_map/reshape | solution.py:183
  81.2 5.3 %copy.80 = bf16[16,49,16,32]{1,3,2,0:T(8,128)(2,1)} copy(bf16[16,49,16,32]{3,2,1,0:T(8,128)(2,1)} %reshape.455) | data formatting | bytes 1605632 | tf_op jit(solution)/shard_map/reshape | solution.py:183
  86.5 4.6 %reshape.454 = bf16[16,49,16,32]{3,2,1,0:T(8,128)(2,1)} reshape(bf16[784,512]{1,0:T(8,128)(2,1)} %get-tuple-element.63) | data formatting | bytes 1605632 | tf_op jit(solution)/shard_map/reshape | solution.py:185
  91.2 5.5 %copy.84 = bf16[16,49,16,32]{1,3,2,0:T(8,128)(2,1)} copy(bf16[16,49,16,32]{3,2,1,0:T(8,128)(2,1)} %reshape.454) | data formatting | bytes 1605632 | tf_op jit(solution)/shard_map/reshape | solution.py:185
  96.7 3.9 fusion.52
  105.0 6.3 %copy.86 = bf16[16,49,16,32]{3,2,0,1:T(8,128)(2,1)} copy(bf16[16,49,16,32]{1,3,2,0:T(8,128)(2,1)S(1)} %convert_bitcast_fusion.1) | data formatting | bytes 1605632 | tf_op jit(solution)/shard_map/convert_element_type | solution.py:190
  111.3 4.5 %reshape_reshape.13 = bf16[1,4,4,7,7,512]{5,2,1,4,3,0:T(4,128)(2,1)S(1)} reshape(bf16[16,49,16,32]{3,2,0,1:T(8,128)(2,1)} %copy.86) | data formatting | bytes 1605632 | tf_op jit(solution)/shard_map/reshape;reshape | solution.py:53
  117.4 4.0 collective-permute-done.2
  122.9 16.7 %all_gather.48 = bf16[512,512]{1,0:T(8,128)(2,1)S(1)} all-gather(bf16[64,512]{1,0:T(8,128)(2,1)S(1)} %copy-done.27), channel_id=1, replica_groups=mesh['seq'=4,'dp'=8] {'dp'}, dimensions={0}, use_global_device_ids=true | all-gather | bytes 589824 | tf_op jit(solution)/shard_map/all_gather | solution.py:145
  139.7 9.4 %all-gather = bf16[8,1,256]{2,1,0:T(2,128)(2,1)S(1)} all-gather(bf16[1,1,256]{2,1,0:T(2,128)(2,1)S(1)} %reshape.426), channel_id=1, replica_groups=mesh['seq'=4,'dp'=8] {'dp'}, dimensions={0}, use_global_device_ids=true | all-gather | bytes 4608 | tf_op jit(solution)/shard_map/all_gather | solution.py:150
  152.9 19.3 %fusion.2 = (bf16[784,2048]{1,0:T(8,128)(2,1)}, f32[784,2048]{1,0:T(8,128)}) fusion(f32[2048]{0:T(1024)S(1)} %bitcast.117, bf16[512,2048]{1,0:T(8,128)(2,1)} %all-gather.7.cloned.1.call-done, f32[784,512]{1,0:T(8,128)S(1)} %get-tuple-element.69, f32[512]{0:T(512)S(1)} %convert_element_type.292, f32[512]{0:T(512)S(1)} %convert_element_type.291, ...), kind=kOutput, calls=%fused_computation.10 | convolution fusion | flops 1752145920 | bytes 13355136 | tf_op jit(solution)/shard_map/dot_general | solution.py:74
  172.2 6.6 %fusion.56 = (bf16[2048]{0:T(1024)(128)(2,1)S(1)}, bf16[784,2048]{1,0:T(8,128)(2,1)S(1)}) fusion(f32[784,2048]{1,0:T(8,128)} %get-tuple-element.71, f32[2048]{0:T(1024)S(1)} %bitcast.118, bf16[2048,512]{1,0:T(8,128)(2,1)} %all-gather.9.cloned.1.call-done, bf16[1,1,784,512]{3,2,1,0:T(8,128)(2,1)S(1)} %copy-done.19), kind=kOutput, calls=%fused_computation.122 | convolution fusion | flops 1663432704 | bytes 12546048 | tf_op jit(solution)/shard_map/dot_general | solution.py:84
  189.7 4.1 collective-permute-done.5
  197.8 6.1 %copy.89 = bf16[16,49,16,32]{1,3,2,0:T(8,128)(2,1)} copy(bf16[16,49,16,32]{3,2,0,1:T(8,128)(2,1)} %reshape_reshape.14) | data formatting | bytes 1605632 | tf_op jit(solution)/shard_map/reshape;reshape | solution.py:248
  203.9 6.0 %fusion.55 = (bf16[16,32]{1,0:T(8,128)(2,1)S(1)}, bf16[16,49,16,32]{1,3,2,0:T(8,128)(2,1)S(1)}) fusion(bf16[16,49,16,32]{1,3,2,0:T(8,128)(2,1)} %copy.89, f32[16,16,49,49]{2,3,1,0:T(8,128)} %copy-done.2, f32[16,16,49]{2,1,0:T(8,128)S(1)} %log_add_fusion), kind=kOutput, calls=%fused_computation.121 | convolution fusion | flops 41369600 | bytes 4115456 | tf_op jit(solution)/shard_map/whqk,wqhe->wkhe/dot_general | solution.py:254
  210.1 5.4 %multiply_reduce_fusion = (f32[16,16,49]{2,1,0:T(8,128)S(1)}, f32[16,16,49,49]{2,3,1,0:T(8,128)}) fusion(f32[16,16,49,49]{2,3,1,0:T(8,128)S(1)} %bitcast.108, f32[16,16,49]{2,1,0:T(8,128)S(1)} %log_add_fusion, bf16[16,49,16,32]{1,3,2,0:T(8,128)(2,1)S(1)} %copy-done.10, bf16[16,49,16,32]{1,3,2,0:T(8,128)(2,1)S(1)} %copy-done.9), kind=kOutput, calls=%fused_computation.4 | convolution fusion | flops 41169408 | bytes 6623232 | tf_op jit(solution)/shard_map/wqhe,wkhe->whqk/dot_general | solution.py:251
  219.5 7.8 %convert_reduce_fusion = (f32[16,49,49]{1,2,0:T(8,128)}, bf16[16,16,49,49]{2,3,1,0:T(8,128)(2,1)S(1)}) fusion(f32[16,16,49,49]{2,3,1,0:T(8,128)} %get-tuple-element.74, f32[16,16,49]{2,1,0:T(8,128)S(1)} %get-tuple-element.73, f32[16,16,49,49]{2,3,1,0:T(8,128)} %copy-done.2, f32[16,16,49]{2,1,0:T(8,128)S(1)} %log_add_fusion), kind=kLoop, calls=%fused_computation.2 | loop fusion | flops 3649520 | bytes 6400576 | tf_op jit(solution)/shard_map/reduce_sum | solution.py:267
  232.0 4.6 %reshape.393 = bf16[784,512]{0,1:T(8,128)(2,1)} reshape(bf16[16,49,16,32]{1,0,3,2:T(8,128)(2,1)} %copy.96) | data formatting | bytes 1605632 | tf_op jit(solution)/shard_map/reshape | solution.py:272
  251.2 5.8 %convolution_convert_fusion.1 = bf16[512,2048]{1,0:T(8,128)(2,1)} fusion(bf16[784,2048]{1,0:T(8,128)(2,1)} %copy-done.18, f32[784,512]{1,0:T(8,128)S(1)} %copy-done.13, f32[512]{0:T(512)S(1)} %convert_element_type.292, f32[512]{0:T(512)S(1)} %convert_element_type.291, f32[784]{0:T(1024)S(1)} %add_rsqrt_fusion, f32[784]{0:T(1024)S(1)} %broadcast_multiply_fusion.4), kind=kOutput, calls=%fused_computation.37 | convolution fusion | flops 1647222784 | bytes 6924416 | tf_op jit(solution)/shard_map/dot_general | solution.py:78
  258.1 5.6 %convolution_convert_fusion = bf16[2048,512]{1,0:T(8,128)(2,1)} fusion(bf16[784,2048]{1,0:T(8,128)(2,1)} %get-tuple-element.70, bf16[1,1,784,512]{3,2,1,0:T(8,128)(2,1)S(1)} %copy-done.20), kind=kOutput, calls=%fused_computation.36 | convolution fusion | flops 1645215744 | bytes 6111232 | tf_op jit(solution)/shard_map/dot_general | solution.py:78
  266.0 4.0 convolution_convert_fusion.3
  271.3 5.0 %reshape.457 = bf16[1,28,28,512]{3,0,2,1:T(2,128)(2,1)} reshape(bf16[1,4,7,4,7,512]{5,4,3,2,1,0:T(8,128)(2,1)} %copy.100) | data formatting | bytes 1605632 | tf_op jit(solution)/shard_map/reshape | solution.py:55
  279.1 3.9 slice.93
  283.2 40.2 %psum.111 = f32[169,16]{0,1:T(8,128)} all-reduce(f32[169,16]{0,1:T(8,128)S(1)} %fusion.17), channel_id=1, replica_groups=mesh['seq'=4,'dp'=8] {'seq','dp'}, use_global_device_ids=true, to_apply=%region_48.49 | all-reduce | flops 2704 | bytes 21632 | tf_op jit(solution)/shard_map/psum | solution.py:343
  331.0 13.1 %multiply_reduce_fusion.2 = (f32[28,28]{1,0:T(8,128)S(1)}, f32[28,28,512]{2,1,0:T(8,128)}, f32[1,28,28,512]{3,0,2,1:T(1,128)}) fusion(f32[512]{0:T(512)S(1)} %copy-done.31, bf16[1,28,25,512]{3,0,2,1:T(2,128)(2,1)S(1)} %get-tuple-element.60, bf16[1,28,3,512]{3,0,2,1:T(2,128)(2,1)S(1)} %collective-permute-done.7), kind=kLoop, calls=%fused_computation.69 | loop fusion | flops 1604848 | bytes 4019264 | tf_op jit(solution)/shard_map/reduce_sum | solution.py:36
  348.9 6.5 %reduce-scatter.11.cloned.1.call-done = bf16[256,512]{1,0:T(8,128)(2,1)} async-done(((bf16[2048,512]{1,0:T(8,128)(2,1)}), bf16[256,512]{1,0:T(8,128)(2,1)}) %reduce-scatter.11.cloned.1.call-update) | async-done | bytes 262160 | tf_op jit(solution)/shard_map/reduce_scatter | solution.py:321
  359.1 26.9 %all-reduce.17 = (bf16[512]{0:T(512)(128)(2,1)S(1)}, bf16[512]{0:T(512)(128)(2,1)S(1)}, bf16[512]{0:T(512)(128)(2,1)S(1)}, bf16[512]{0:T(512)(128)(2,1)S(1)}, bf...) all-reduce(bf16[512]{0:T(512)(128)(2,1)S(1)} %dynamic-update-slice., ...), channel_id=1, replica_groups=mesh['seq'=4,'dp'=8] {'dp'}, use_global_device_ids=true, to_apply=%add.7 | all-reduce | flops 6656 | bytes 26624
  386.6 9.8 %all-reduce.19 = (bf16[64]{0:T(256)(128)(2,1)S(1)}, bf16[64]{0:T(256)(128)(2,1)S(1)}, bf16[64]{0:T(256)(128)(2,1)S(1)}, bf16[64]{0:T(256)(128)(2,1)S(1)}, bf16[6...) all-reduce(bf16[64]{0:T(256)(128)(2,1)S(1)} %dynamic-slice.9, ...), channel_id=1, replica_groups=mesh['seq'=4,'dp'=8] {'seq'}, use_global_device_ids=true, to_apply=%region_13.14 | all-reduce | flops 768 | bytes 3072 | tf_op jit(solution)/shard_map/psum | solution.py:329
  401.2 5.4 %fusion.36 = bf16[1,1,784,512]{3,2,1,0:T(8,128)(2,1)} fusion(f32[784,512]{1,0:T(8,128)S(1)} %copy-done.13, bf16[784,2048]{1,0:T(8,128)(2,1)} %get-tuple-element.70, bf16[2048,512]{1,0:T(8,128)(2,1)} %all-gather.9.cloned.1.call-done, f32[512]{0:T(512)S(1)} %convert_element_type.296), kind=kOutput, calls=%fused_computation.82 | convolution fusion | flops 1645371392 | bytes 7718912 | tf_op jit(solution)/shard_map/dot_general | solution.py:74
  (262 shorter events, 124.6 us)
Async XLA Ops:
  7.2 42.8 %copy-start = (f32[169,16]{0,1:T(8,128)S(1)}, f32[169,16]{0,1:T(8,128)}, u32[]{:S(2)}) copy-start(f32[169,16]{0,1:T(8,128)} %param.33) | copy-start | bytes 32452
  7.2 31.4 %copy-start.4 = (bf16[1,1,784,512]{3,2,1,0:T(8,128)(2,1)S(1)}, bf16[1,1,784,512]{3,2,1,0:T(8,128)(2,1)}, u32[]{:S(2)}) copy-start(bf16[1,1,784,512]{3,2,1,0:T(8,128)(2,1)} %param.18) | copy-start | bytes 2408452
  7.2 56.6 %all-gather.5.cloned.1.call-start = ((), (), s32[]{:S(2)}) async-start(), calls=%async_computation.4 | async-start | bytes 1769472 | tf_op jit(solution)/shard_map/all_gather | solution.py:142
  7.9 144.9 %all-gather.7.cloned.1.call-start = ((), (), s32[]{:S(2)}) async-start(), calls=%async_computation.5 | async-start | bytes 2359296 | tf_op jit(solution)/shard_map/all_gather | solution.py:149
  35.5 6.7 %copy-start.30 = (f32[512]{0:T(512)}, f32[512]{0:T(512)S(1)}, u32[]{:S(2)}) copy-start(f32[512]{0:T(512)S(1)} %convert_element_type.282) | copy-start | bytes 6148
  39.4 8.7 %copy-start.28 = (f32[784]{0:T(1024)}, f32[784]{0:T(1024)S(1)}, u32[]{:S(2)}) copy-start(f32[784]{0:T(1024)S(1)} %add_rsqrt_fusion.1) | copy-start | bytes 9412
  43.5 9.8 %collective-permute-start = (bf16[1,3,28,512]{3,0,2,1:T(2,128)(2,1)S(1)}, bf16[1,3,28,512]{3,0,2,1:T(2,128)(2,1)S(1)}, u32[]{:S(2)}, u32[]{:S(2)}) collective-permute-start(bf16[1,3,28,512]{3,0,2,1:T(2,128)(2,1)S(1)} %slice.80), channel_id=1, source_target_pairs={{0,8},{8,0},{16,24},{24,16},{1,9},{9,1},{17,25},{25,17},{2,10},{10... | collective-permute-start | bytes 258056 | tf_op jit(solution)/shard_map/ppermute | solution.py:16
  45.2 127.0 %all-gather.9.cloned.1.call-start = ((), (), s32[]{:S(2)}) async-start(), calls=%async_computation.6 | async-start | bytes 2359296 | tf_op jit(solution)/shard_map/all_gather | solution.py:151
  53.6 5.5 %collective-permute-start.1 = (bf16[1,28,3,512]{3,0,2,1:T(2,128)(2,1)S(1)}, bf16[1,28,3,512]{3,0,2,1:T(2,128)(2,1)S(1)}, u32[]{:S(2)}, u32[]{:S(2)}) collective-permute-start(bf16[1,28,3,512]{3,0,2,1:T(2,128)(2,1)S(1)} %pad_maximum_fusion.4), channel_id=1, source_target_pairs={{0,16},{8,24},{16,0},{24,8},{1,17},{9,25},{17,1},{25,9},{2,18},{10... | collective-permute-start | bytes 258056 | tf_op jit(solution)/shard_map/ppermute | solution.py:22
  76.3 20.4 %copy-start.6 = (bf16[16,49,16,32]{1,3,2,0:T(8,128)(2,1)}, bf16[16,49,16,32]{1,3,2,0:T(8,128)(2,1)S(1)}, u32[]{:S(2)}) copy-start(bf16[16,49,16,32]{1,3,2,0:T(8,128)(2,1)S(1)} %copy.81) | copy-start | bytes 2408452
  116.6 23.1 %copy-start.40 = (bf16[256]{0:T(256)(128)(2,1)S(1)}, bf16[256]{0:T(256)(128)(2,1)}, u32[]{:S(2)}) copy-start(bf16[256]{0:T(256)(128)(2,1)} %param.30) | copy-start | bytes 1540
  116.6 23.0 %copy-start.38 = (bf16[512]{0:T(512)(128)(2,1)S(1)}, bf16[512]{0:T(512)(128)(2,1)}, u32[]{:S(2)}) copy-start(bf16[512]{0:T(512)(128)(2,1)} %get-tuple-element.40) | copy-start | bytes 3076
  116.6 23.1 %copy-start.37 = (bf16[512]{0:T(512)(128)(2,1)S(1)}, bf16[512]{0:T(512)(128)(2,1)}, u32[]{:S(2)}) copy-start(bf16[512]{0:T(512)(128)(2,1)} %get-tuple-element.39) | copy-start | bytes 3076
  116.6 23.1 %copy-start.36 = (bf16[512]{0:T(512)(128)(2,1)S(1)}, bf16[512]{0:T(512)(128)(2,1)}, u32[]{:S(2)}) copy-start(bf16[512]{0:T(512)(128)(2,1)} %get-tuple-element.38) | copy-start | bytes 3076
  116.7 4.7 %collective-permute-start.2 = (bf16[1,3,28,512]{3,2,1,0:T(8,128)(2,1)S(1)}, bf16[1,3,28,512]{3,2,1,0:T(8,128)(2,1)S(1)}, u32[]{:S(2)}, u32[]{:S(2)}) collective-permute-start(bf16[1,3,28,512]{3,2,1,0:T(8,128)(2,1)S(1)} %slice.86), channel_id=1, source_target_pairs={{0,8},{8,0},{16,24},{24,16},{1,9},{9,1},{17,25},{25,17},{2,10},{10... | collective-permute-start | bytes 258056 | tf_op jit(solution)/shard_map/ppermute | solution.py:16
  117.3 231.6 %reduce-scatter.7.cloned.1.call-start = ((), (), s32[]{:S(2)}) async-start(), calls=%async_computation.8 | async-start | bytes 589824 | tf_op jit(solution)/shard_map/reduce_scatter | solution.py:303
  121.4 27.7 %collective-permute-start.3 = (bf16[1,28,3,512]{3,2,1,0:T(4,128)(2,1)S(1)}, bf16[1,28,3,512]{3,2,1,0:T(4,128)(2,1)S(1)}, u32[]{:S(2)}, u32[]{:S(2)}) collective-permute-start(bf16[1,28,3,512]{3,2,1,0:T(4,128)(2,1)S(1)} %pad_maximum_fusion.6), channel_id=1, source_target_pairs={{0,16},{8,24},{16,0},{24,8},{1,17},{9,25},{17,1},{25,9},{2,18},{10... | collective-permute-start | bytes 258056 | tf_op jit(solution)/shard_map/ppermute | solution.py:22
  152.5 28.7 %copy-start.12 = (f32[784,512]{1,0:T(8,128)}, f32[784,512]{1,0:T(8,128)S(1)}, u32[]{:S(2)}) copy-start(f32[784,512]{1,0:T(8,128)S(1)} %get-tuple-element.69) | copy-start | bytes 4816900
  152.9 19.3 %copy-start.19 = (bf16[1,1,784,512]{3,2,1,0:T(8,128)(2,1)S(1)}, bf16[1,1,784,512]{3,2,1,0:T(8,128)(2,1)}, u32[]{:S(2)}) copy-start(bf16[1,1,784,512]{3,2,1,0:T(8,128)(2,1)} %param.19) | copy-start | bytes 2408452
  183.8 5.1 %collective-permute-start.4 = (bf16[1,3,28,512]{3,2,1,0:T(8,128)(2,1)S(1)}, bf16[1,3,28,512]{3,2,1,0:T(8,128)(2,1)S(1)}, u32[]{:S(2)}, u32[]{:S(2)}) collective-permute-start(bf16[1,3,28,512]{3,2,1,0:T(8,128)(2,1)S(1)} %slice.89), channel_id=1, source_target_pairs={{0,8},{8,0},{16,24},{24,16},{1,9},{9,1},{17,25},{25,17},{2,10},{10... | collective-permute-start | bytes 258056 | tf_op jit(solution)/shard_map/ppermute | solution.py:16
  187.6 161.3 %reduce-scatter.5.cloned.1.call-start = ((), (), s32[]{:S(2)}) async-start(), calls=%async_computation.7 | async-start | bytes 1769472 | tf_op jit(solution)/shard_map/reduce_scatter | solution.py:294
  189.0 4.9 %collective-permute-start.5 = (bf16[1,28,3,512]{3,2,1,0:T(4,128)(2,1)S(1)}, bf16[1,28,3,512]{3,2,1,0:T(4,128)(2,1)S(1)}, u32[]{:S(2)}, u32[]{:S(2)}) collective-permute-start(bf16[1,28,3,512]{3,2,1,0:T(4,128)(2,1)S(1)} %pad_maximum_fusion.5), channel_id=1, source_target_pairs={{0,16},{8,24},{16,0},{24,8},{1,17},{9,25},{17,1},{25,9},{2,18},{10... | collective-permute-start | bytes 258056 | tf_op jit(solution)/shard_map/ppermute | solution.py:22
  197.8 12.1 %slice-start = ((s8[7340032]{0:T(1024)(128)(4,1)}), s8[3145728]{0:T(1024)(128)(4,1)S(1)}, s32[]{:S(2)}) async-start(s8[7340032]{0:T(1024)(128)(4,1)} %bitcast.107), calls=%async_computation.12 | async-start | bytes 6291456
  219.4 7.8 %copy-start.11 = (bf16[16,49,16,32]{1,3,2,0:T(8,128)(2,1)S(1)}, bf16[16,49,16,32]{1,3,2,0:T(8,128)(2,1)}, u32[]{:S(2)}) copy-start(bf16[16,49,16,32]{1,3,2,0:T(8,128)(2,1)} %copy.80) | copy-start | bytes 2408452
  250.9 98.1 %reduce-scatter.9.cloned.1.call-start = ((), (), s32[]{:S(2)}) async-start(), calls=%async_computation.9 | async-start | bytes 2359296 | tf_op jit(solution)/shard_map/reduce_scatter | solution.py:315
  257.0 98.5 %reduce-scatter.11.cloned.1.call-start = ((), (), s32[]{:S(2)}) async-start(), calls=%async_computation.10 | async-start | bytes 2359296 | tf_op jit(solution)/shard_map/reduce_scatter | solution.py:321
  263.8 143.5 %all-reduce.23.cloned.1.call-start = ((), (), s32[]{:S(2)}) async-start(), calls=%async_computation.11 | async-start | bytes 1572864 | tf_op jit(solution)/shard_map/psum | solution.py:331
  270.3 7.9 %copy-start.34 = (s32[2401]{0:T(1024)S(1)}, s32[2401]{0:T(1024)}, u32[]{:S(2)}) copy-start(s32[2401]{0:T(1024)} %copy-done.33) | copy-start | bytes 28816
  277.5 45.9 %collective-permute-start.6 = (bf16[1,3,28,512]{3,0,2,1:T(2,128)(2,1)S(1)}, bf16[1,3,28,512]{3,0,2,1:T(2,128)(2,1)S(1)}, u32[]{:S(2)}, u32[]{:S(2)}) collective-permute-start(bf16[1,3,28,512]{3,0,2,1:T(2,128)(2,1)S(1)} %slice.92), channel_id=1, source_target_pairs={{0,8},{8,0},{16,24},{24,16},{1,9},{9,1},{17,25},{25,17},{2,10},{10... | collective-permute-start | bytes 258056 | tf_op jit(solution)/shard_map/ppermute | solution.py:16
  323.4 7.6 %copy-start.31 = (f32[512]{0:T(512)S(1)}, f32[512]{0:T(512)}, u32[]{:S(2)}) copy-start(f32[512]{0:T(512)} %copy-done.30) | copy-start | bytes 6148
  324.6 6.3 %collective-permute-start.7 = (bf16[1,28,3,512]{3,0,2,1:T(2,128)(2,1)S(1)}, bf16[1,28,3,512]{3,0,2,1:T(2,128)(2,1)S(1)}, u32[]{:S(2)}, u32[]{:S(2)}) collective-permute-start(bf16[1,28,3,512]{3,0,2,1:T(2,128)(2,1)S(1)} %pad_maximum_fusion.3), channel_id=1, source_target_pairs={{0,16},{8,24},{16,0},{24,8},{1,17},{9,25},{17,1},{25,9},{2,18},{10... | collective-permute-start | bytes 258056 | tf_op jit(solution)/shard_map/ppermute | solution.py:22
  401.2 12.9 %copy-start.1 = (f32[169,16]{0,1:T(8,128)S(1)}, f32[169,16]{0,1:T(8,128)}, u32[]{:S(2)}) copy-start(f32[169,16]{0,1:T(8,128)} %param.33) | copy-start | bytes 32452
  (28 other events, 92.5 us)
Sparse Core Ops, SparseCore 0:
  9.7 28.1 all-gather.4
  45.3 26.3 all-gather.6
  117.4 30.5 all-gather.8
  187.7 29.1 reduce-scatter.6
  251.0 31.4 reduce-scatter.4
  284.8 33.9 reduce-scatter.8
  321.2 34.2 reduce-scatter.10
  359.2 48.0 all-reduce.22
where the time goes:
time: 430 us; the launch traced here: 421 us
  blocking collectives  123 us (29%)
  local copies, waits for them, and re-layouts  108 us (25%)
  matrix products  84.4 us (20%)
  other arithmetic  60.2 us (14%)
  waiting for transfers between devices  18.8 us (4%)
  between operations  17.5 us (4%)
  starting transfers between devices  10.2 us (2%)
    unnamed x2, blocking collectives  46.4 us
    psum x1, blocking collectives, local(): table_total = lax.psum(grad_table, ('seq', 'dp'))  40.2 us
    dot_general x4, matrix products, matmul_plain(): return jnp.dot(left, right, preferred_element_type=jnp.float32)  29.3 us
    dot_general x4, matrix products, left_inner(): lax.dot_general(left, right, (((0,), (0,)), ((), ())), preferred_element_...  17.7 us
    unnamed x117, local copies, waits for them, and re-layouts  17.1 us
    all_gather x1, blocking collectives, local(): lax.all_gather(proj_weight, 'dp', axis=0, tiled=True)  16.7 us
    dot_general x4, matrix products, right_inner(): lax.dot_general(left, right, (((1,), (1,)), ((), ())), preferred_element_...  13.5 us
    reduce_sum x1, other arithmetic, normalize_back(): jnp.mean(inner, -1, keepdims=True)  13.1 us
  transfers between devices with their start and end apart: 16, of which 7 were waited for; matrix products, arithmetic and copies ran while one was open for 54% of the time, Pallas kernels for 0%

commit v1 on v0

v1 whole, which is shorter than its diff:
```python
import functools

import jax
import jax.numpy as jnp
from jax import lax
from jax.experimental import pallas as pl
from jax.experimental.pallas import tpu as pltpu
from jax.sharding import PartitionSpec as P

HIGHEST = lax.Precision.HIGHEST
F32 = jnp.float32
BF16 = jnp.bfloat16
SIDE = 7
CELLS = SIDE * SIDE
ROWS = 56
PAIR = 2 * ROWS
VMEM = 56 * 1024 * 1024


def send(value, rows, cols):
    count = lax.axis_size("seq")
    wide = count // 2
    pairs = []
    for place in range(count):
        r, c = place % 2, place // 2
        source = (c + cols) % wide * 2 + (r + rows) % 2
        pairs.append((source, place))
    return lax.ppermute(value, "seq", pairs)


def roll_ahead(field):
    below = send(field[:, :3, 3:], 1, 0)
    beside = send(field[:, 3:, :3], 0, 1)
    corner = send(field[:, :3, :3], 1, 1)
    top = jnp.concatenate([field[:, 3:, 3:], beside], 2)
    low = jnp.concatenate([below, corner], 2)
    return jnp.concatenate([top, low], 1)


def roll_behind(field):
    above = send(field[:, -3:, :-3], -1, 0)
    beside = send(field[:, :-3, -3:], 0, -1)
    corner = send(field[:, -3:, -3:], -1, -1)
    top = jnp.concatenate([corner, above], 2)
    low = jnp.concatenate([beside, field[:, :-3, :-3]], 2)
    return jnp.concatenate([top, low], 1)


def to_windows(field):
    batch, rows, cols, width = field.shape
    return (
        field.reshape(batch, rows // SIDE, SIDE, cols // SIDE, SIDE, width)
        .transpose(0, 1, 3, 2, 4, 5)
        .reshape(-1, CELLS, width)
    )


def from_windows(blocks, batch, rows, cols):
    width = blocks.shape[-1]
    return (
        blocks.reshape(batch, rows // SIDE, cols // SIDE, SIDE, SIDE, width)
        .transpose(0, 1, 3, 2, 4, 5)
        .reshape(batch, rows, cols, width)
    )


def pad_windows(field):
    return jnp.pad(to_windows(field), ((0, 0), (0, ROWS - CELLS), (0, 0))).reshape(
        -1, field.shape[-1]
    )


def stack_heads(block, per):
    part = lax.broadcasted_iota(jnp.int32, block.shape, 1) // (block.shape[1] // per)
    return jnp.concatenate([jnp.where(part == j, block, jnp.zeros_like(block)) for j in range(per)], 0)


def merge_heads(tall, per):
    rows = tall.shape[0] // per
    part = lax.broadcasted_iota(jnp.int32, (rows, tall.shape[1]), 1) // (tall.shape[1] // per)
    total = jnp.where(part == 0, tall[:rows], 0.0)
    for j in range(1, per):
        total = jnp.where(part == j, tall[j * rows : (j + 1) * rows], total)
    return total


def dot_nt(left, right):
    return lax.dot_general(left, right, (((1,), (1,)), ((), ())), preferred_element_type=F32)


def dot_tn(left, right):
    return lax.dot_general(left, right, (((0,), (0,)), ((), ())), preferred_element_type=F32)


def dot_nn(left, right):
    return jnp.dot(left, right, preferred_element_type=F32)


def attend_kernel(scale, per, qkv_ref, bias_ref, mask_ref, o_ref, p_ref):
    dim = o_ref.shape[1]
    tall = per * PAIR
    mask = mask_ref[0]
    for g in range(dim // 128):
        at = slice(g * 128, (g + 1) * 128)
        band = slice(g * tall, (g + 1) * tall)
        q = stack_heads(qkv_ref[:, g * 128 : (g + 1) * 128], per)
        k = qkv_ref[:, dim + g * 128 : dim + (g + 1) * 128]
        v = qkv_ref[:, 2 * dim + g * 128 : 2 * dim + (g + 1) * 128]
        s = dot_nt(q, k) * scale + bias_ref[band, :]
        s = (s.reshape(per, PAIR, PAIR) + mask[None]).reshape(tall, PAIR)
        e = jnp.exp(s - jnp.max(s, -1, keepdims=True))
        p = (e * (1.0 / jnp.sum(e, -1, keepdims=True))).astype(BF16)
        p_ref[0, band, :] = p
        o_ref[:, at] = merge_heads(dot_nn(p, v), per).astype(BF16)


def attend_back_kernel(scale, per, qkv_ref, do_ref, p_ref, dqkv_ref, sum_ref):
    dim = do_ref.shape[1]
    tall = per * PAIR

    @pl.when(pl.program_id(0) == 0)
    def _():
        sum_ref[...] = jnp.zeros_like(sum_ref)

    for g in range(dim // 128):
        band = slice(g * tall, (g + 1) * tall)
        q = stack_heads(qkv_ref[:, g * 128 : (g + 1) * 128], per)
        k = qkv_ref[:, dim + g * 128 : dim + (g + 1) * 128]
        v = qkv_ref[:, 2 * dim + g * 128 : 2 * dim + (g + 1) * 128]
        do = stack_heads(do_ref[:, g * 128 : (g + 1) * 128], per)
        p = p_ref[0, band, :]
        pf = p.astype(F32)
        dp = dot_nt(do, v)
        dl = (pf * (dp - jnp.sum(dp * pf, -1, keepdims=True))).astype(BF16)
        sum_ref[band, :] += dl.astype(F32)
        dq = merge_heads(dot_nn(dl, k), per) * scale
        dk = dot_tn(dl, q) * scale
        dv = dot_tn(p, do)
        dqkv_ref[:, g * 128 : (g + 1) * 128] = dq.astype(BF16)
        dqkv_ref[:, dim + g * 128 : dim + (g + 1) * 128] = dk.astype(BF16)
        dqkv_ref[:, 2 * dim + g * 128 : 2 * dim + (g + 1) * 128] = dv.astype(BF16)


def attend(qkv, bias, mask, heads):
    rows, dim = qkv.shape[0], qkv.shape[1] // 3
    pairs = rows // PAIR
    per = 128 * heads // dim
    return pl.pallas_call(
        functools.partial(attend_kernel, (dim // heads) ** -0.5, per),
        grid=(pairs,),
        out_shape=(
            jax.ShapeDtypeStruct((rows, dim), BF16),
            jax.ShapeDtypeStruct((pairs, heads * PAIR, PAIR), BF16),
        ),
        in_specs=[
            pl.BlockSpec((PAIR, 3 * dim), lambda i: (i, 0)),
            pl.BlockSpec((heads * PAIR, PAIR), lambda i: (0, 0)),
            pl.BlockSpec((1, PAIR, PAIR), lambda i: (i, 0, 0)),
        ],
        out_specs=(
            pl.BlockSpec((PAIR, dim), lambda i: (i, 0)),
            pl.BlockSpec((1, heads * PAIR, PAIR), lambda i: (i, 0, 0)),
        ),
        compiler_params=pltpu.CompilerParams(vmem_limit_bytes=VMEM),
        cost_estimate=pl.CostEstimate(
            flops=4 * rows * heads * PAIR * 128, bytes_accessed=rows * dim * 8, transcendentals=rows * heads * 128
        ),
    )(qkv, bias, mask)


def attend_back(qkv, grad, probs, heads):
    rows, dim = grad.shape
    pairs = rows // PAIR
    per = 128 * heads // dim
    return pl.pallas_call(
        functools.partial(attend_back_kernel, (dim // heads) ** -0.5, per),
        grid=(pairs,),
        out_shape=(
            jax.ShapeDtypeStruct((rows, 3 * dim), BF16),
            jax.ShapeDtypeStruct((heads * PAIR, PAIR), F32),
        ),
        in_specs=[
            pl.BlockSpec((PAIR, 3 * dim), lambda i: (i, 0)),
            pl.BlockSpec((PAIR, dim), lambda i: (i, 0)),
            pl.BlockSpec((1, heads * PAIR, PAIR), lambda i: (i, 0, 0)),
        ],
        out_specs=(
            pl.BlockSpec((PAIR, 3 * dim), lambda i: (i, 0)),
            pl.BlockSpec((heads * PAIR, PAIR), lambda i: (0, 0)),
        ),
        compiler_params=pltpu.CompilerParams(vmem_limit_bytes=VMEM),
        cost_estimate=pl.CostEstimate(
            flops=8 * rows * heads * PAIR * 128, bytes_accessed=rows * dim * 16, transcendentals=0
        ),
    )(qkv, grad, probs)


def normalize(values):
    center = values - jnp.mean(values, -1, keepdims=True)
    scaled = lax.rsqrt(jnp.mean(center * center, -1, keepdims=True) + 1e-05)
    return center * scaled, scaled


def normalize_back(grad, unit, scaled, gain):
    inner = grad * gain
    return scaled * (
        inner
        - jnp.mean(inner, -1, keepdims=True)
        - unit * jnp.mean(inner * unit, -1, keepdims=True)
    )


def gather_rows(weight):
    share = weight.shape[0] // lax.axis_size("seq")
    mine = lax.dynamic_slice_in_dim(weight, lax.axis_index("seq") * share, share, 0)
    return lax.all_gather(mine, ("dp", "seq"), axis=0, tiled=True)


def reduce_rows(grad):
    part = lax.psum_scatter(grad.astype(BF16), ("dp", "seq"), scatter_dimension=0, tiled=True)
    return lax.all_gather(part, "seq", axis=0, tiled=True).astype(F32)


def local(
    tokens,
    cotangent,
    norm1_gain,
    norm1_bias,
    qkv_weight,
    query_bias,
    value_bias,
    proj_weight,
    proj_bias,
    norm2_gain,
    norm2_bias,
    fc1_weight,
    fc1_bias,
    fc2_weight,
    fc2_bias,
    bias_table,
    region_ids,
    rel_index,
):
    batch = tokens.shape[0]
    dim = tokens.shape[-1]
    heads = bias_table.shape[1]
    image_rows, image_cols = region_ids.shape
    seq_count = lax.axis_size("seq")
    tile_rows = image_rows // 2
    tile_cols = image_cols * 2 // seq_count
    place = lax.axis_index("seq")

    smalls = [
        norm1_gain, norm1_bias, query_bias, value_bias, proj_bias, norm2_gain, norm2_bias, fc2_bias, fc1_bias,
    ]
    small_all = lax.all_gather(jnp.concatenate(smalls), "dp", axis=0, tiled=False)
    full, at = [], 0
    for s in smalls:
        full.append(small_all[:, at : at + s.shape[0]].reshape(-1).astype(F32))
        at += s.shape[0]
    gain_one, shift_one, qbias, vbias, pbias, gain_two, shift_two, fc2b, fc1b = full
    qkv_full = gather_rows(qkv_weight)
    proj_full = gather_rows(proj_weight)
    fc1_full = gather_rows(fc1_weight)
    fc2_full = gather_rows(fc2_weight)

    regions = lax.dynamic_slice(
        region_ids, (place % 2 * tile_rows, place // 2 * tile_cols), (tile_rows, tile_cols)
    )
    region_win = to_windows(regions[None, :, :, None])[:, :, 0]
    mask = jnp.where(region_win[:, :, None] == region_win[:, None, :], 0.0, -100.0).astype(F32)
    mask = jnp.tile(mask, (batch, 1, 1))
    low = -1e30
    mask = jnp.pad(mask, ((0, 0), (0, 0), (0, ROWS - CELLS)), constant_values=low)
    mask = jnp.pad(mask, ((0, 0), (0, ROWS - CELLS), (0, 0)))
    mask = mask.at[:, CELLS:, CELLS:].set(low)
    mask = mask.reshape(-1, 2, ROWS, ROWS)
    other = jnp.full_like(mask[:, 0], low)
    mask = jnp.concatenate(
        [jnp.concatenate([mask[:, 0], other], 2), jnp.concatenate([other, mask[:, 1]], 2)], 1
    )
    onehot = (
        rel_index.reshape(-1)[:, None] == jnp.arange(bias_table.shape[0], dtype=jnp.int32)[None, :]
    ).astype(F32)
    bias = jnp.dot(onehot, bias_table, precision=HIGHEST).reshape(CELLS, CELLS, heads).transpose(2, 0, 1)
    bias = jnp.pad(bias, ((0, 0), (0, ROWS - CELLS), (0, ROWS - CELLS)))
    bias = jnp.tile(bias, (1, 2, 2)).reshape(heads * PAIR, PAIR)

    source = pad_windows(roll_ahead(tokens.reshape(batch, tile_rows, tile_cols, dim)))
    grad_out = pad_windows(roll_ahead(cotangent.reshape(batch, tile_rows, tile_cols, dim)))
    source = source.astype(F32)

    unit_one, scaled_one = normalize(source)
    first = (unit_one * gain_one + shift_one).astype(BF16)
    qkv_bias = jnp.concatenate([qbias, jnp.zeros((dim,), F32), vbias])
    qkv = (dot_nn(first, qkv_full) + qkv_bias).astype(BF16)
    mixed, probs = attend(qkv, bias, mask, heads)
    resid = source + dot_nn(mixed, proj_full) + pbias
    unit_two, scaled_two = normalize(resid)
    second = (unit_two * gain_two + shift_two).astype(BF16)
    before = dot_nn(second, fc1_full) + fc1b
    normal_cdf = 0.5 * (1.0 + lax.erf(before * 0.7071067811865476))
    hidden = (before * normal_cdf).astype(BF16)
    output = (resid + dot_nn(hidden, fc2_full) + fc2b).astype(BF16)

    def to_tile(field):
        field = field.reshape(-1, ROWS, dim)[:, :CELLS]
        return roll_behind(from_windows(field, batch, tile_rows, tile_cols)).reshape(tokens.shape)

    output = to_tile(output)

    grad_fc2 = dot_tn(hidden, grad_out)
    grad_fc2b = jnp.sum(grad_out.astype(F32), 0)
    grad_hidden = dot_nt(grad_out, fc2_full)
    normal_pdf = jnp.exp(-0.5 * before * before) * 0.3989422804014327
    grad_before = (grad_hidden * (normal_cdf + before * normal_pdf)).astype(BF16)
    grad_fc1 = dot_tn(second, grad_before)
    grad_fc1b = jnp.sum(grad_before.astype(F32), 0)
    grad_second = dot_nt(grad_before, fc1_full)
    grad_gain2 = jnp.sum(grad_second * unit_two, 0)
    grad_shift2 = jnp.sum(grad_second, 0)
    grad_resid = grad_out.astype(F32) + normalize_back(grad_second, unit_two, scaled_two, gain_two)
    grad_pbias = jnp.sum(grad_resid, 0)
    grad_branch = grad_resid.astype(BF16)
    grad_proj = dot_tn(mixed, grad_branch)
    grad_mixed = dot_nt(grad_branch, proj_full).astype(BF16)
    grad_qkv_rows, score_sum = attend_back(qkv, grad_mixed, probs, heads)
    score_sum = score_sum.reshape(heads, PAIR, PAIR)
    score_sum = score_sum[:, :CELLS, :CELLS] + score_sum[:, ROWS : ROWS + CELLS, ROWS : ROWS + CELLS]
    grad_table = jnp.dot(
        onehot.T, score_sum.transpose(1, 2, 0).reshape(-1, heads), precision=HIGHEST
    )
    grad_qkv = dot_tn(first, grad_qkv_rows)
    grad_qkvb = jnp.sum(grad_qkv_rows.astype(F32), 0)
    grad_first = dot_nt(grad_qkv_rows, qkv_full).astype(BF16).astype(F32)
    grad_gain1 = jnp.sum(grad_first * unit_one, 0)
    grad_shift1 = jnp.sum(grad_first, 0)
    input_grad = normalize_back(grad_first, unit_one, scaled_one, gain_one) + grad_resid
    input_grad = to_tile(input_grad.astype(BF16))

    sum_fc2 = reduce_rows(grad_fc2)
    sum_fc1 = reduce_rows(grad_fc1)
    sum_proj = reduce_rows(grad_proj)
    sum_qkv = reduce_rows(grad_qkv)
    count = lax.axis_size("dp")
    vectors = [
        grad_gain1, grad_shift1, grad_qkvb[:dim], grad_qkvb[2 * dim :], grad_pbias, grad_gain2,
        grad_shift2, grad_fc2b, grad_fc1b,
    ]
    joined = lax.psum(jnp.concatenate(vectors + [grad_table.reshape(-1)]), ("dp", "seq"))
    owned, at = [], 0
    for v in vectors:
        size = v.shape[0] // count
        owned.append(lax.dynamic_slice(joined, (at + lax.axis_index("dp") * size,), (size,)))
        at += v.shape[0]
    table_total = joined[at:].reshape(bias_table.shape)
    s_gain1, s_shift1, s_qb, s_vb, s_pb, s_gain2, s_shift2, s_fc2b, s_fc1b = owned
    return (
        output,
        input_grad,
        s_gain1,
        s_shift1,
        sum_qkv,
        s_qb,
        s_vb,
        sum_proj,
        s_pb,
        s_gain2,
        s_shift2,
        sum_fc1,
        s_fc1b,
        sum_fc2,
        s_fc2b,
        table_total,
    )


def solution(mesh):
    rows, vector, matrix, whole = P("dp", "seq", None, None), P("dp"), P("dp", None), P()
    params = (
        vector, vector, matrix, vector, vector, matrix, vector, vector, vector, matrix, vector, matrix, vector,
    )
    in_specs = (rows, rows) + params + (whole, whole, whole)
    out_specs = (rows, rows) + params + (whole,)
    return jax.shard_map(local, mesh=mesh, in_specs=in_specs, out_specs=out_specs, check_vma=False)
```

time: 430 us -> 732 us (1.70)
  waiting for transfers between devices: 18.8 us -> 385 us
  local copies, waits for them, and re-layouts: 108 us -> 48 us
  other arithmetic: 60.2 us -> 16.6 us
  blocking collectives: 123 us -> 158 us
  Pallas kernels: 0 us -> 25.8 us
  matrix products: 84.4 us -> 60.7 us
    reduce_scatter x4, waiting for transfers between devices: 6.59 us -> 360 us  [reduce_rows(): lax.psum_scatter(grad.astype(BF16), ('dp', 'seq'), scatter_dimension=0, t...]
    all_gather x2 -> x6, blocking collectives: 26.1 us -> 118 us  [the longest x1 71.2 us: gather_rows(): return lax.all_gather(mine, ('dp', 'seq'), axis=0, tiled=True)]
    unnamed x2 -> x0, blocking collectives: 46.4 us -> none
    reshape x16 -> x17, local copies, waits for them, and re-layouts: 45.4 us -> 14.7 us  [the longest x4 6.73 us: from_windows(): blocks.reshape(batch, rows // SIDE, cols // SIDE, SIDE, SIDE, width)]
    reduce_sum x8 -> x2, other arithmetic: 27.8 us -> 1.2 us  [the longest x1 0.76 us: local(): grad_fc2b = jnp.sum(grad_out.astype(F32), 0)]
    pallas_call x0 -> x2, Pallas kernels: none -> 25.8 us  [the longest x1 14.8 us: attend_back(): pl.pallas_call(functools.partial(attend_back_kernel, (dim // heads) ** (-...]
    dot_general x19 -> x13, matrix products: 83.5 us -> 58.8 us  [the longest x4 20.7 us: dot_nn(): return jnp.dot(left, right, preferred_element_type=F32)]
    all_gather x3, waiting for transfers between devices: 0.04 us -> 22.8 us  [gather_rows(): return lax.all_gather(mine, ('dp', 'seq'), axis=0, tiled=True)]
  transfers between devices with their start and end apart: 16 -> 19, of which waited for: 7 -> 7; matrix products, arithmetic and copies ran while one was open for 54% -> 15% of each run, Pallas kernels for 0% -> 4%
where the time goes in v1:
time: 732 us; the launch traced here: 725 us
  waiting for transfers between devices  385 us (53%)
  blocking collectives  158 us (22%)
  matrix products  60.7 us (8%)
  local copies, waits for them, and re-layouts  48 us (7%)
  Pallas kernels  25.8 us (4%)
  other arithmetic  16.6 us (2%)
  starting transfers between devices  15.9 us (2%)
  between operations  15.6 us (2%)
    reduce_scatter x4, waiting for transfers between devices, reduce_rows(): lax.psum_scatter(grad.astype(BF16), ('dp', 'seq'), scatter_dimension=0, t...  360 us
    all_gather x1, blocking collectives, gather_rows(): return lax.all_gather(mine, ('dp', 'seq'), axis=0, tiled=True)  71.2 us
    psum x1, blocking collectives, local(): lax.psum(jnp.concatenate(vectors + [grad_table.reshape(-1)]), ('dp', 'seq'))  39.2 us
    all_gather x4, blocking collectives, reduce_rows(): return lax.all_gather(part, 'seq', axis=0, tiled=True).astype(F32)  33.1 us
    all_gather x3, waiting for transfers between devices, gather_rows(): return lax.all_gather(mine, ('dp', 'seq'), axis=0, tiled=True)  22.8 us
    dot_general x4, matrix products, dot_nn(): return jnp.dot(left, right, preferred_element_type=F32)  20.7 us
    dot_general x4, matrix products, dot_tn(): lax.dot_general(left, right, (((0,), (0,)), ((), ())), preferred_element_...  18.8 us
    dot_general x4, matrix products, dot_nt(): lax.dot_general(left, right, (((1,), (1,)), ((), ())), preferred_element_...  18 us
  transfers between devices with their start and end apart: 19, of which 7 were waited for; matrix products, arithmetic and copies ran while one was open for 15% of the time, Pallas kernels for 4%

profile of v1, /device:TPU:0, one launch (start us, length us, event | category | flops | bytes accessed | tf_op | source)
XLA Modules:
  0.0 725.2 jit_solution(11449719718255807307)
XLA Ops:
  11.6 3.9 collective-permute-start.2
  17.6 2.9 collective-permute-start.8
  23.5 14.1 %all-gather.1 = bf16[8,1,768]{2,1,0:T(2,128)(2,1)S(1)} all-gather(bf16[1,1,768]{2,1,0:T(2,128)(2,1)S(1)} %reshape.302), channel_id=2, replica_groups=mesh['seq'=4,'dp'=8] {'dp'}, dimensions={0}, use_global_device_ids=true | all-gather | bytes 13824 | tf_op jit(solution)/shard_map/all_gather | solution.py:256
  38.4 4.9 scatter.4
  46.4 71.2 %all_gather.33 = bf16[512,512]{1,0:T(8,128)(2,1)S(1)} all-gather(bf16[16,512]{1,0:T(8,128)(2,1)S(1)} %constant_dynamic-slice_fusion.2), channel_id=1, replica_groups=mesh['seq'=4,'dp'=8] {'dp','seq'}, dimensions={0}, use_global_device_ids=true | all-gather | bytes 540672 | tf_op jit(solution)/shard_map/all_gather | solution.py:216
  122.0 2.9 tile.9
  137.9 4.8 add_convert_fusion.qkv_ref
  142.7 11.1 %shard_map.297 = (bf16[896,512]{1,0:T(8,128)(2,1)}, bf16[8,1792,112]{2,1,0:T(8,128)(2,1)}) custom-call(bf16[896,1536]{1,0:T(8,128)(2,1)} %add_convert_fusion.qkv_ref, f32[1792,112]{1,0:T(8,128)} %copy.94.bias_ref, f32[8,112,112]{2,1,0:T(8,128)} %select_maximum_fusion.mask_ref), custom_call_target="tpu_custom_call" | custom-call | flops 822083584 | bytes 3670016 | tf_op jit(solution)/shard_map/pallas_call | solution.py:148
  153.8 1.9 fusion.29
  157.4 7.7 %multiply_convert_fusion = (bf16[896,2048]{1,0:T(8,128)(2,1)}, f32[896,2048]{1,0:T(8,128)}) fusion(f32[2048]{0:T(1024)S(1)} %bitcast.102, bf16[512,2048]{1,0:T(8,128)(2,1)} %all-gather.8.cloned.1.call-done, f32[896,512]{1,0:T(8,128)} %copy-done.4, f32[512]{0:T(512)S(1)} %reshape.298, f32[512]{0:T(512)S(1)} %reshape.297, f32[896]{0:T(1024)S(1)} %add_rsqrt_fusion.1, ...), kind=kOutput, calls=%fused_computation.8 | convolution fusion | flops 1892352000 | bytes 14961664 | tf_op jit(solution)/shard_map/dot_general | solution.py:96
  165.1 22.8 %all-gather.10.cloned.1.call-done = bf16[2048,512]{1,0:T(8,128)(2,1)} async-done(((bf16[64,512]{1,0:T(8,128)(2,1)}), bf16[2048,512]{1,0:T(8,128)(2,1)}) %all-gather.10.cloned.1.call-update) | async-done | bytes 2097168 | tf_op jit(solution)/shard_map/all_gather | solution.py:216
  188.0 8.3 %convert_reduce_fusion = (f32[2048]{0:T(1024)}, bf16[896,2048]{1,0:T(8,128)(2,1)S(1)}) fusion(f32[896,2048]{1,0:T(8,128)} %get-tuple-element.135, f32[2048]{0:T(1024)S(1)} %bitcast.103, bf16[896,512]{1,0:T(8,128)(2,1)S(1)} %bitcast.92, bf16[2048,512]{1,0:T(8,128)(2,1)} %all-gather.10.cloned.1.call-done), kind=kOutput, calls=%fused_computation.7 | convolution fusion | flops 1902901248 | bytes 14041088 | tf_op jit(solution)/shard_map/dot_general | solution.py:88
  196.2 3.1 multiply_reduce_fusion
  204.0 14.8 %shard_map.298 = (bf16[896,1536]{1,0:T(8,128)(2,1)}, f32[1792,112]{1,0:T(8,128)}) custom-call(bf16[896,1536]{1,0:T(8,128)(2,1)} %add_convert_fusion.qkv_ref, bf16[896,512]{1,0:T(8,128)(2,1)} %convolution_convert_fusion.4.do_ref, bf16[8,1792,112]{2,1,0:T(8,128)(2,1)} %get-tuple-element.33.p_ref), custom_call_target="tpu_custom_call" | custom-call | flops 1644167168 | bytes 7340032 | tf_op jit(solution)/shard_map/pallas_call | solution.py:175
  218.8 4.7 convolution_convert_fusion.2
  223.6 6.1 convolution_convert_fusion
  230.9 6.5 convolution_convert_fusion.1
  237.4 6.3 add_convert_fusion.1
  254.2 1.9 fusion.19
  256.2 5.0 fusion.16
  262.9 2.3 reshape.306
  265.3 2.6 copy.117
  268.4 39.2 %psum.7 = f32[8848]{0:T(1024)S(1)} all-reduce(f32[8848]{0:T(1024)S(1)} %constant_dynamic-update-slice_fusion), channel_id=1, replica_groups=mesh['seq'=4,'dp'=8] {'dp','seq'}, use_global_device_ids=true, to_apply=%region_16.17 | all-reduce | flops 8848 | bytes 70784 | tf_op jit(solution)/shard_map/psum | solution.py:350
  310.3 3.0 collective-permute-start.9
  321.9 13.6 %reduce-scatter.7.cloned.1.call-done = bf16[16,512]{1,0:T(8,128)(2,1)} async-done(((bf16[512,512]{1,0:T(8,128)(2,1)}), bf16[16,512]{1,0:T(8,128)(2,1)}) %reduce-scatter.7.cloned.1.call-update) | async-done | bytes 16400 | tf_op jit(solution)/shard_map/reduce_scatter | solution.py:220
  335.5 7.4 %all_gather.37 = bf16[64,512]{1,0:T(8,128)(2,1)S(1)} all-gather(bf16[16,512]{1,0:T(8,128)(2,1)} %reduce-scatter.7.cloned.1.call-done), channel_id=1, replica_groups=mesh['seq'=4,'dp'=8] {'seq'}, dimensions={0}, use_global_device_ids=true | all-gather | bytes 81920 | tf_op jit(solution)/shard_map/all_gather | solution.py:221
  343.5 91.5 %reduce-scatter.5.cloned.1.call-done = bf16[16,1536]{1,0:T(8,128)(2,1)} async-done(((bf16[512,1536]{1,0:T(8,128)(2,1)}), bf16[16,1536]{1,0:T(8,128)(2,1)}) %reduce-scatter.5.cloned.1.call-update) | async-done | bytes 49168 | tf_op jit(solution)/shard_map/reduce_scatter | solution.py:220
  435.1 8.8 %all_gather.36 = bf16[64,1536]{1,0:T(8,128)(2,1)S(1)} all-gather(bf16[16,1536]{1,0:T(8,128)(2,1)} %reduce-scatter.5.cloned.1.call-done), channel_id=1, replica_groups=mesh['seq'=4,'dp'=8] {'seq'}, dimensions={0}, use_global_device_ids=true | all-gather | bytes 245760 | tf_op jit(solution)/shard_map/all_gather | solution.py:221
  444.6 128.8 %reduce-scatter.11.cloned.1.call-done = bf16[64,512]{1,0:T(8,128)(2,1)} async-done(((bf16[2048,512]{1,0:T(8,128)(2,1)}), bf16[64,512]{1,0:T(8,128)(2,1)}) %reduce-scatter.11.cloned.1.call-update) | async-done | bytes 65552 | tf_op jit(solution)/shard_map/reduce_scatter | solution.py:220
  573.4 8.6 %all_gather.39 = bf16[256,512]{1,0:T(8,128)(2,1)S(1)} all-gather(bf16[64,512]{1,0:T(8,128)(2,1)} %reduce-scatter.11.cloned.1.call-done), channel_id=1, replica_groups=mesh['seq'=4,'dp'=8] {'seq'}, dimensions={0}, use_global_device_ids=true | all-gather | bytes 327680 | tf_op jit(solution)/shard_map/all_gather | solution.py:221
  582.9 125.8 %reduce-scatter.9.cloned.1.call-done = bf16[16,2048]{1,0:T(8,128)(2,1)} async-done(((bf16[512,2048]{1,0:T(8,128)(2,1)}), bf16[16,2048]{1,0:T(8,128)(2,1)}) %reduce-scatter.9.cloned.1.call-update) | async-done | bytes 65552 | tf_op jit(solution)/shard_map/reduce_scatter | solution.py:220
  708.7 8.3 %all_gather.38 = bf16[64,2048]{1,0:T(8,128)(2,1)S(1)} all-gather(bf16[16,2048]{1,0:T(8,128)(2,1)} %reduce-scatter.9.cloned.1.call-done), channel_id=1, replica_groups=mesh['seq'=4,'dp'=8] {'seq'}, dimensions={0}, use_global_device_ids=true | all-gather | bytes 327680 | tf_op jit(solution)/shard_map/all_gather | solution.py:221
  (232 shorter events, 64.7 us)
Async XLA Ops:
  7.2 130.7 %all-gather.6.cloned.1.call-start = ((), (), s32[]{:S(2)}) async-start(), calls=%async_computation.4 | async-start | bytes 1622016 | tf_op jit(solution)/shard_map/all_gather | solution.py:216
  8.8 148.6 %all-gather.8.cloned.1.call-start = ((), (), s32[]{:S(2)}) async-start(), calls=%async_computation.5 | async-start | bytes 2162688 | tf_op jit(solution)/shard_map/all_gather | solution.py:216
  9.5 13.7 %copy-start.26 = (bf16[64]{0:T(256)(128)(2,1)S(1)}, bf16[64]{0:T(256)(128)(2,1)}, u32[]{:S(2)}) copy-start(bf16[64]{0:T(256)(128)(2,1)} %param.22) | copy-start | bytes 388
  9.5 13.7 %copy-start.27 = (bf16[64]{0:T(256)(128)(2,1)S(1)}, bf16[64]{0:T(256)(128)(2,1)}, u32[]{:S(2)}) copy-start(bf16[64]{0:T(256)(128)(2,1)} %param.23) | copy-start | bytes 388
  9.6 13.7 %copy-start.28 = (bf16[64]{0:T(256)(128)(2,1)S(1)}, bf16[64]{0:T(256)(128)(2,1)}, u32[]{:S(2)}) copy-start(bf16[64]{0:T(256)(128)(2,1)} %param.25) | copy-start | bytes 388
  9.6 13.7 %copy-start.29 = (bf16[64]{0:T(256)(128)(2,1)S(1)}, bf16[64]{0:T(256)(128)(2,1)}, u32[]{:S(2)}) copy-start(bf16[64]{0:T(256)(128)(2,1)} %param.26) | copy-start | bytes 388
  9.6 13.7 %copy-start.30 = (bf16[64]{0:T(256)(128)(2,1)S(1)}, bf16[64]{0:T(256)(128)(2,1)}, u32[]{:S(2)}) copy-start(bf16[64]{0:T(256)(128)(2,1)} %param.28) | copy-start | bytes 388
  9.6 13.7 %copy-start.31 = (bf16[64]{0:T(256)(128)(2,1)S(1)}, bf16[64]{0:T(256)(128)(2,1)}, u32[]{:S(2)}) copy-start(bf16[64]{0:T(256)(128)(2,1)} %param.29) | copy-start | bytes 388
  9.6 28.0 %copy-start.17 = (s32[49,49]{1,0:T(8,128)S(1)}, s32[49,49]{1,0:T(8,128)}, u32[]{:S(2)}) copy-start(s32[49,49]{1,0:T(8,128)} %param.37) | copy-start | bytes 28816
  9.7 178.3 %all-gather.10.cloned.1.call-start = ((), (), s32[]{:S(2)}) async-start(), calls=%async_computation.6 | async-start | bytes 2162688 | tf_op jit(solution)/shard_map/all_gather | solution.py:216
  11.0 26.9 %copy-start.20 = (s32[56,56]{1,0:T(8,128)S(1)}, s32[56,56]{1,0:T(8,128)}, u32[]{:S(2)}) copy-start(s32[56,56]{1,0:T(8,128)} %param.36) | copy-start | bytes 37636
  11.6 114.6 %collective-permute-start.2 = (bf16[1,3,3,512]{3,2,1,0:T(4,128)(2,1)}, bf16[1,3,3,512]{3,2,1,0:T(4,128)(2,1)S(1)}, u32[]{:S(2)}, u32[]{:S(2)}) collective-permute-start(bf16[1,3,3,512]{3,2,1,0:T(4,128)(2,1)} %slice.173), channel_id=1, source_target_pairs={{24,0},{16,8},{8,16},{0,24},{25,1},{17,9},{9,17},{1,25},{26,2},{18... | collective-permute-start | bytes 27656 | tf_op jit(solution)/shard_map/ppermute | solution.py:28
  16.1 110.0 %collective-permute-start.1 = (bf16[1,3,25,512]{3,2,1,0:T(8,128)(2,1)}, bf16[1,3,25,512]{3,2,1,0:T(8,128)(2,1)}, u32[]{:S(2)}, u32[]{:S(2)}) collective-permute-start(bf16[1,3,25,512]{3,2,1,0:T(8,128)(2,1)} %slice.172), channel_id=1, source_target_pairs={{8,0},{0,8},{24,16},{16,24},{9,1},{1,9},{25,17},{17,25},{10,2},{2,... | collective-permute-start | bytes 230408 | tf_op jit(solution)/shard_map/ppermute | solution.py:28
  16.7 109.4 %collective-permute-start = (bf16[1,25,3,512]{3,2,1,0:T(4,128)(2,1)S(1)}, bf16[1,25,3,512]{3,2,1,0:T(4,128)(2,1)}, u32[]{:S(2)}, u32[]{:S(2)}) collective-permute-start(bf16[1,25,3,512]{3,2,1,0:T(4,128)(2,1)S(1)} %slice.171), channel_id=1, source_target_pairs={{16,0},{24,8},{0,16},{8,24},{17,1},{25,9},{1,17},{9,25},{18,2},{26... | collective-permute-start | bytes 230408 | tf_op jit(solution)/shard_map/ppermute | solution.py:28
  17.0 26.4 %copy-start.36 = (f32[169,16]{0,1:T(8,128)S(1)}, f32[169,16]{0,1:T(8,128)}, u32[]{:S(2)}) copy-start(f32[169,16]{0,1:T(8,128)} %param.35) | copy-start | bytes 32452
  17.6 114.1 %collective-permute-start.8 = (bf16[1,3,3,512]{3,2,1,0:T(4,128)(2,1)}, bf16[1,3,3,512]{3,2,1,0:T(4,128)(2,1)S(1)}, u32[]{:S(2)}, u32[]{:S(2)}) collective-permute-start(bf16[1,3,3,512]{3,2,1,0:T(4,128)(2,1)} %slice.193), channel_id=1, source_target_pairs={{24,0},{16,8},{8,16},{0,24},{25,1},{17,9},{9,17},{1,25},{26,2},{18... | collective-permute-start | bytes 27656 | tf_op jit(solution)/shard_map/ppermute | solution.py:28
  21.2 110.6 %collective-permute-start.7 = (bf16[1,3,25,512]{3,2,1,0:T(8,128)(2,1)}, bf16[1,3,25,512]{3,2,1,0:T(8,128)(2,1)}, u32[]{:S(2)}, u32[]{:S(2)}) collective-permute-start(bf16[1,3,25,512]{3,2,1,0:T(8,128)(2,1)} %slice.192), channel_id=1, source_target_pairs={{8,0},{0,8},{24,16},{16,24},{9,1},{1,9},{25,17},{17,25},{10,2},{2,... | collective-permute-start | bytes 230408 | tf_op jit(solution)/shard_map/ppermute | solution.py:28
  23.2 312.3 %reduce-scatter.7.cloned.1.call-start = ((), (), s32[]{:S(2)}) async-start(), calls=%async_computation.8 | async-start | bytes 540672 | tf_op jit(solution)/shard_map/reduce_scatter | solution.py:220
  126.1 5.6 collective-permute-start.6
  135.5 18.2 %copy-start.2 = (f32[16,56,512]{2,1,0:T(8,128)}, f32[16,56,512]{2,1,0:T(8,128)S(1)}, u32[]{:S(2)}) copy-start(f32[16,56,512]{2,1,0:T(8,128)S(1)} %copy.86) | copy-start | bytes 5505028
  157.4 30.5 %copy-start.11 = (bf16[16,56,512]{2,1,0:T(8,128)(2,1)S(1)}, bf16[16,56,512]{2,1,0:T(8,128)(2,1)}, u32[]{:S(2)}) copy-start(bf16[16,56,512]{2,1,0:T(8,128)(2,1)} %pad.29.clone) | copy-start | bytes 2752516
  202.4 232.7 %reduce-scatter.5.cloned.1.call-start = ((), (), s32[]{:S(2)}) async-start(), calls=%async_computation.7 | async-start | bytes 1622016 | tf_op jit(solution)/shard_map/reduce_scatter | solution.py:220
  204.0 14.8 %copy-start.10 = (bf16[896,512]{1,0:T(8,128)(2,1)S(1)}, bf16[896,512]{1,0:T(8,128)(2,1)}, u32[]{:S(2)}) copy-start(bf16[896,512]{1,0:T(8,128)(2,1)} %add_convert_fusion.3) | copy-start | bytes 2752516
  223.6 349.9 %reduce-scatter.11.cloned.1.call-start = ((), (), s32[]{:S(2)}) async-start(), calls=%async_computation.10 | async-start | bytes 2162688 | tf_op jit(solution)/shard_map/reduce_scatter | solution.py:220
  229.7 479.0 %reduce-scatter.9.cloned.1.call-start = ((), (), s32[]{:S(2)}) async-start(), calls=%async_computation.9 | async-start | bytes 2162688 | tf_op jit(solution)/shard_map/reduce_scatter | solution.py:220
  249.1 66.5 %collective-permute-start.3 = (bf16[1,3,3,512]{3,2,1,0:T(4,128)(2,1)S(1)}, bf16[1,3,3,512]{3,2,1,0:T(4,128)(2,1)S(1)}, u32[]{:S(2)}, u32[]{:S(2)}) collective-permute-start(bf16[1,3,3,512]{3,2,1,0:T(4,128)(2,1)S(1)} %slice.186), channel_id=1, source_target_pairs={{24,0},{16,8},{8,16},{0,24},{25,1},{17,9},{9,17},{1,25},{26,2},{18... | collective-permute-start | bytes 27656 | tf_op jit(solution)/shard_map/ppermute | solution.py:28
  250.6 65.0 %collective-permute-start.4 = (bf16[1,3,25,512]{3,2,1,0:T(8,128)(2,1)}, bf16[1,3,25,512]{3,2,1,0:T(8,128)(2,1)}, u32[]{:S(2)}, u32[]{:S(2)}) collective-permute-start(bf16[1,3,25,512]{3,2,1,0:T(8,128)(2,1)} %slice.187), channel_id=1, source_target_pairs={{8,0},{0,8},{24,16},{16,24},{9,1},{1,9},{25,17},{17,25},{10,2},{2,... | collective-permute-start | bytes 230408 | tf_op jit(solution)/shard_map/ppermute | solution.py:28
  252.0 63.6 %collective-permute-start.5 = (bf16[1,25,3,512]{3,2,1,0:T(4,128)(2,1)S(1)}, bf16[1,25,3,512]{3,2,1,0:T(4,128)(2,1)}, u32[]{:S(2)}, u32[]{:S(2)}) collective-permute-start(bf16[1,25,3,512]{3,2,1,0:T(4,128)(2,1)S(1)} %slice.188), channel_id=1, source_target_pairs={{16,0},{24,8},{0,16},{8,24},{17,1},{25,9},{1,17},{9,25},{18,2},{26... | collective-permute-start | bytes 230408 | tf_op jit(solution)/shard_map/ppermute | solution.py:28
  310.3 7.8 %collective-permute-start.9 = (bf16[1,3,3,512]{3,2,1,0:T(4,128)(2,1)S(1)}, bf16[1,3,3,512]{3,2,1,0:T(4,128)(2,1)S(1)}, u32[]{:S(2)}, u32[]{:S(2)}) collective-permute-start(bf16[1,3,3,512]{3,2,1,0:T(4,128)(2,1)S(1)} %slice.195), channel_id=1, source_target_pairs={{24,0},{16,8},{8,16},{0,24},{25,1},{17,9},{9,17},{1,25},{26,2},{18... | collective-permute-start | bytes 27656 | tf_op jit(solution)/shard_map/ppermute | solution.py:28
  314.8 4.8 collective-permute-start.10
  315.6 4.7 collective-permute-start.11
  320.8 397.0 %copy-start.1 = (bf16[64,2048]{1,0:T(8,128)(2,1)S(1)}, bf16[64,2048]{1,0:T(8,128)(2,1)}, u32[]{:S(2)}) copy-start(bf16[64,2048]{1,0:T(8,128)(2,1)} %param.31) | copy-start | bytes 786436
  (24 other events, 139.8 us)
Sparse Core Ops, SparseCore 0:
  10.9 58.2 all-gather.5
  72.7 57.0 all-gather.7
  133.2 54.7 all-gather.9
  202.5 132.9 reduce-scatter.6
  341.4 93.6 reduce-scatter.4
  437.3 136.0 reduce-scatter.10
  575.7 132.9 reduce-scatter.8

commit v2 on v1

--- a/solution.py
+++ b/solution.py
@@ -17,33 +17,268 @@
 VMEM = 56 * 1024 * 1024
 
 
-def send(value, rows, cols):
-    count = lax.axis_size("seq")
-    wide = count // 2
-    pairs = []
-    for place in range(count):
-        r, c = place % 2, place // 2
-        source = (c + cols) % wide * 2 + (r + rows) % 2
-        pairs.append((source, place))
-    return lax.ppermute(value, "seq", pairs)
-
-
-def roll_ahead(field):
-    below = send(field[:, :3, 3:], 1, 0)
-    beside = send(field[:, 3:, :3], 0, 1)
-    corner = send(field[:, :3, :3], 1, 1)
-    top = jnp.concatenate([field[:, 3:, 3:], beside], 2)
-    low = jnp.concatenate([below, corner], 2)
-    return jnp.concatenate([top, low], 1)
-
-
-def roll_behind(field):
-    above = send(field[:, -3:, :-3], -1, 0)
-    beside = send(field[:, :-3, -3:], 0, -1)
-    corner = send(field[:, -3:, -3:], -1, -1)
-    top = jnp.concatenate([corner, above], 2)
-    low = jnp.concatenate([beside, field[:, :-3, :-3]], 2)
-    return jnp.concatenate([top, low], 1)
+MESH = pl.DeviceIdType.MESH
+TILE = 16
+STEP = 3
+
+
+def edges_ahead(field):
+    return field[:, :STEP, STEP:], field[:, STEP:, :STEP], field[:, :STEP, :STEP]
+
+
+def edges_behind(field):
+    return field[:, -STEP:, :-STEP], field[:, :-STEP, -STEP:], field[:, -STEP:, -STEP:]
+
+
+def join_ahead(field, below, beside, corner):
+    top = jnp.concatenate([field[:, STEP:, STEP:], beside], 2)
+    return jnp.concatenate([top, jnp.concatenate([below, corner], 2)], 1)
+
+
+def join_behind(field, above, beside, corner):
+    low = jnp.concatenate([beside, field[:, :-STEP, :-STEP]], 2)
+    return jnp.concatenate([jnp.concatenate([corner, above], 2), low], 1)
+
+
+def pack_edges(edges):
+    packed = []
+    for blocks in zip(*edges):
+        rows = jnp.concatenate([b.reshape(-1, b.shape[-1]) for b in blocks], 0)
+        packed.append(jnp.pad(rows, ((0, -rows.shape[0] % TILE), (0, 0))))
+    return packed
+
+
+def unpack_edges(packed, edges):
+    fields = [[] for _ in edges]
+    for rows, blocks in zip(packed, zip(*edges)):
+        at = 0
+        for field, b in zip(fields, blocks):
+            size = b.size // b.shape[-1]
+            field.append(rows[at : at + size].reshape(b.shape))
+            at += size
+    return fields
+
+
+class Mail:
+    def __init__(self, send, recv):
+        self.send, self.recv, self.used, self.open = send, recv, 0, []
+
+    def push(self, src, dst, seq, dp):
+        copy = pltpu.make_async_remote_copy(
+            src_ref=src,
+            dst_ref=dst,
+            send_sem=self.send.at[self.used],
+            recv_sem=self.recv.at[self.used],
+            device_id=(seq, dp),
+            device_id_type=MESH,
+        )
+        copy.start()
+        self.used += 1
+        self.open.append(copy)
+        return copy
+
+    def close(self):
+        for copy in self.open:
+            copy.wait_send()
+
+
+def places(n, nd):
+    s, d = lax.axis_index("seq"), lax.axis_index("dp")
+    core = d % 2
+    row = s + 1 - 2 * (s % 2)
+    col = (s + 2) % n
+    one = (1 - core) * row + core * col
+    two = core * row + (1 - core) * col
+    return s, d, one, two, (s // 2 * 2 + 2) % n + 1 - s % 2
+
+
+def greet(n, nd, s, d):
+    barrier = pltpu.get_barrier_semaphore()
+    for m in range(1, n):
+        pl.semaphore_signal(barrier, inc=1, device_id=((s + m) % n, d), device_id_type=MESH)
+    for m in range(1, nd):
+        pl.semaphore_signal(barrier, inc=1, device_id=(s, (d + m) % nd), device_id_type=MESH)
+    pl.semaphore_wait(barrier, n - 1 + nd - 1)
+
+
+def edge_sends(mail, n, s, d, src, dst, cols):
+    row = s + 1 - 2 * (s % 2)
+    col = (s + 2 * cols + n) % n
+    return [
+        mail.push(src[0], dst[0], row, d),
+        mail.push(src[1], dst[1], col, d),
+        mail.push(src[2], dst[2], col + 1 - 2 * (col % 2), d),
+    ]
+
+
+def gather_kernel(n, nd, w_ref, e0, e1, e2, o_ref, f0, f1, f2, send, recv, own):
+    s, d, one, two, far = places(n, nd)
+    nz, core = nd // 2, d % 2
+    z = d // 2
+    mate = d + 1 - 2 * core
+    quarter = w_ref.shape[0] // n
+
+    def part(block, q):
+        return o_ref.at[block, pl.ds(pl.multiple_of(q * quarter, TILE), quarter)]
+
+    greet(n, nd, s, d)
+    mail = Mail(send, recv)
+    keep = pltpu.make_async_copy(w_ref, o_ref.at[d], own)
+    keep.start()
+    mine = w_ref.at[pl.ds(pl.multiple_of(s * quarter, TILE), quarter)]
+    along = [mail.push(mine, part(d, s), s, (z + k) % nz * 2 + core) for k in range(1, nz)]
+    waits = edge_sends(mail, n, s, d, (e0, e1, e2), (f0, f1, f2), -1)
+    waits.append(mail.push(w_ref, o_ref.at[d], s, mate))
+    blocks = [(z + nz - k) % nz * 2 + core for k in range(1, nz)]
+    across = []
+    for copy, block in zip(along, blocks):
+        copy.wait_recv()
+        piece = part(block, s)
+        if n == 4:
+            across.append([(mail.push(piece, piece, one, d), one), (mail.push(piece, piece, two, d), two)])
+        else:
+            across.append(
+                [(mail.push(piece, piece, (s + m) % n, d), (s + n - m) % n) for m in range(1, n)]
+            )
+        waits.append(mail.push(piece, piece, s, mate))
+    for group, block in zip(across, blocks):
+        for at, (copy, source) in enumerate(group):
+            copy.wait_recv()
+            piece = part(block, source)
+            if n == 4 and at == 0:
+                group.append((mail.push(piece, piece, two, d), far))
+            waits.append(mail.push(piece, piece, s, mate))
+    for copy in waits:
+        copy.wait_recv()
+    mail.close()
+    keep.wait()
+
+
+def gather_all(shard, edges, n, nd):
+    count = (nd // 2 - 1) * (1 + (n if n != 4 else 4) - 1 + n) + 4
+    any_spec = pl.BlockSpec(memory_space=pl.ANY)
+    shapes = [jax.ShapeDtypeStruct((nd,) + shard.shape, shard.dtype)]
+    shapes += [jax.ShapeDtypeStruct(e.shape, e.dtype) for e in edges]
+    return pl.pallas_call(
+        functools.partial(gather_kernel, n, nd),
+        out_shape=shapes,
+        in_specs=[any_spec] * 4,
+        out_specs=[any_spec] * 4,
+        scratch_shapes=[
+            pltpu.SemaphoreType.DMA((count,)),
+            pltpu.SemaphoreType.DMA((count,)),
+            pltpu.SemaphoreType.DMA,
+        ],
+        compiler_params=pltpu.CompilerParams(collective_id=0, has_side_effects=True),
+    )(shard, *edges)
+
+
+def reduce_kernel(n, nd, low, g_ref, e0, e1, e2, o_ref, t_ref, f0, f1, f2, held, ra, rb, mid, q_ref, rc, send, recv, own):
+    s, d, one, two, far = places(n, nd)
+    nz, core = nd // 2, d % 2
+    z = d // 2
+    mate = d + 1 - 2 * core
+    quarter = o_ref.shape[0] // n
+
+    def rows(q):
+        return pl.ds(pl.multiple_of(q * quarter, TILE), quarter)
+
+    greet(n, nd, s, d)
+    mail = Mail(send, recv)
+    order = list(range(1, nz)) + [0]
+    first = [
+        mail.push(g_ref.at[(z + k) % nz * 2 + 1 - core], ra.at[k], s, mate) for k in order
+    ]
+    second = []
+    for k, copy in zip(order, first):
+        copy.wait_recv()
+        held[k] = g_ref[(z + k) % nz * 2 + core] + ra[k]
+        if n == 4:
+            second.append(
+                [
+                    mail.push(held.at[k, rows(far)], rb.at[k, 0], one, d),
+                    mail.push(held.at[k, rows(one)], rb.at[k, 1], one, d),
+                ]
+            )
+        else:
+            second.append(
+                [
+                    mail.push(held.at[k, rows((s + m) % n)], rb.at[k, m - 1], (s + m) % n, d)
+                    for m in range(1, n)
+                ]
+            )
+    if n == 4:
+        for k, group in zip(order, second):
+            group[0].wait_recv()
+            mid[k] = held[k, rows(two)] + rb[k, 0]
+            group.append(mail.push(mid.at[k], rb.at[k, 2], two, d))
+    edge = edge_sends(mail, n, s, d, (e0, e1, e2), (f0, f1, f2), 1)
+    third = []
+    for k, group in zip(order, second):
+        total = held[k, rows(s)].astype(F32)
+        for at in range(1 if n == 4 else 0, n - 1):
+            group[at].wait_recv()
+            total = total + rb[k, at].astype(F32)
+        q_ref[k] = total.astype(BF16)
+        if k:
+            third.append(mail.push(q_ref.at[k], rc.at[k - 1], s, (z + k) % nz * 2 + core))
+    total = q_ref[0].astype(F32)
+    for k, copy in enumerate(third):
+        copy.wait_recv()
+        total = total + rc[k].astype(F32)
+    o_ref[rows(s)] = total.astype(BF16)
+    mine = o_ref.at[rows(s)]
+    if n == 4:
+        a, b = mail.push(mine, mine, one, d), mail.push(mine, mine, two, d)
+        a.wait_recv()
+        block = o_ref.at[rows(one)]
+        last = [b, mail.push(block, block, two, d)]
+    else:
+        last = [mail.push(mine, mine, (s + m) % n, d) for m in range(1, n)]
+    for copy in last:
+        copy.wait_recv()
+    table = o_ref.at[pl.ds(low, TILE)]
+    keep = pltpu.make_async_copy(table, t_ref.at[d], own)
+    keep.start()
+    tables = [mail.push(table, t_ref.at[d], s, (d + m) % nd) for m in range(1, nd)]
+    for copy in tables + edge:
+        copy.wait_recv()
+    mail.close()
+    keep.wait()
+
+
+def reduce_all(grads, edges, low, n, nd):
+    nz = nd // 2
+    rows, width = grads.shape[1:]
+    quarter = rows // n
+    count = nz * 4 + nz * n + n + nd + 8
+    any_spec = pl.BlockSpec(memory_space=pl.ANY)
+    vmem_spec = pl.BlockSpec(memory_space=pltpu.VMEM)
+    shapes = [
+        jax.ShapeDtypeStruct((rows, width), BF16),
+        jax.ShapeDtypeStruct((nd, TILE, width), BF16),
+    ]
+    shapes += [jax.ShapeDtypeStruct(e.shape, e.dtype) for e in edges]
+    return pl.pallas_call(
+        functools.partial(reduce_kernel, n, nd, low),
+        out_shape=shapes,
+        in_specs=[vmem_spec] + [any_spec] * 3,
+        out_specs=[vmem_spec, vmem_spec] + [any_spec] * 3,
+        scratch_shapes=[
+            pltpu.VMEM((nz, rows, width), BF16),
+            pltpu.VMEM((nz, rows, width), BF16),
+            pltpu.VMEM((nz, n - 1, quarter, width), BF16),
+            pltpu.VMEM((nz, quarter, width), BF16),
+            pltpu.VMEM((nz, quarter, width), BF16),
+            pltpu.VMEM((nz - 1 if nz > 1 else 1, quarter, width), BF16),
+            pltpu.SemaphoreType.DMA((count,)),
+            pltpu.SemaphoreType.DMA((count,)),
+            pltpu.SemaphoreType.DMA,
+        ],
+        compiler_params=pltpu.CompilerParams(
+            collective_id=1, has_side_effects=True, vmem_limit_bytes=VMEM
+        ),
+    )(grads, *edges)
 
 
 def to_windows(field):
@@ -208,17 +443,6 @@
         - jnp.mean(inner, -1, keepdims=True)
         - unit * jnp.mean(inner * unit, -1, keepdims=True)
     )
-
-
-def gather_rows(weight):
-    share = weight.shape[0] // lax.axis_size("seq")
-    mine = lax.dynamic_slice_in_dim(weight, lax.axis_index("seq") * share, share, 0)
-    return lax.all_gather(mine, ("dp", "seq"), axis=0, tiled=True)
-
-
-def reduce_rows(grad):
-    part = lax.psum_scatter(grad.astype(BF16), ("dp", "seq"), scatter_dimension=0, tiled=True)
-    return lax.all_gather(part, "seq", axis=0, tiled=True).astype(F32)
 
 
 def local(
@@ -250,19 +474,48 @@
     tile_cols = image_cols * 2 // seq_count
     place = lax.axis_index("seq")
 
+    count = lax.axis_size("dp")
+    share = dim // count
+    wide = fc1_weight.shape[1] // dim
+
     smalls = [
         norm1_gain, norm1_bias, query_bias, value_bias, proj_bias, norm2_gain, norm2_bias, fc2_bias, fc1_bias,
     ]
-    small_all = lax.all_gather(jnp.concatenate(smalls), "dp", axis=0, tiled=False)
+    low = share * (4 + 2 * wide)
+    total_rows = -(-(low + TILE) // (TILE * seq_count)) * TILE * seq_count
+    tail = total_rows - low
+    short = jnp.concatenate(smalls)
+    small_size = short.shape[0]
+    short = jnp.pad(short, (0, tail * dim - small_size)).reshape(tail, dim)
+
+    def columns(matrix):
+        return [matrix[:, at : at + dim] for at in range(0, matrix.shape[1], dim)]
+
+    shard = jnp.concatenate(
+        columns(qkv_weight) + [proj_weight] + columns(fc1_weight) + [fc2_weight, short], 0
+    )
+    tile = tokens.reshape(batch, tile_rows, tile_cols, dim)
+    grad_tile = cotangent.reshape(batch, tile_rows, tile_cols, dim)
+    edges = [edges_ahead(tile), edges_ahead(grad_tile)]
+    gathered, *blocks = gather_all(shard, pack_edges(edges), seq_count, count)
+    blocks = unpack_edges(blocks, edges)
+
+    def matrix_of(at, blocks_wide):
+        parts = [
+            gathered[:, at + j * share : at + (j + 1) * share].reshape(dim, dim) for j in range(blocks_wide)
+        ]
+        return parts[0] if blocks_wide == 1 else jnp.concatenate(parts, 1)
+
+    qkv_full = matrix_of(0, 3)
+    proj_full = matrix_of(3 * share, 1)
+    fc1_full = matrix_of(4 * share, wide)
+    fc2_full = gathered[:, (4 + wide) * share : low].reshape(-1, dim)
+    small_all = gathered[:, low:].reshape(count, -1)
     full, at = [], 0
-    for s in smalls:
-        full.append(small_all[:, at : at + s.shape[0]].reshape(-1).astype(F32))
-        at += s.shape[0]
+    for v in smalls:
+        full.append(small_all[:, at : at + v.shape[0]].reshape(-1).astype(F32))
+        at += v.shape[0]
     gain_one, shift_one, qbias, vbias, pbias, gain_two, shift_two, fc2b, fc1b = full
-    qkv_full = gather_rows(qkv_weight)
-    proj_full = gather_rows(proj_weight)
-    fc1_full = gather_rows(fc1_weight)
-    fc2_full = gather_rows(fc2_weight)
 
     regions = lax.dynamic_slice(
         region_ids, (place % 2 * tile_rows, place // 2 * tile_cols), (tile_rows, tile_cols)
@@ -270,12 +523,12 @@
     region_win = to_windows(regions[None, :, :, None])[:, :, 0]
     mask = jnp.where(region_win[:, :, None] == region_win[:, None, :], 0.0, -100.0).astype(F32)
     mask = jnp.tile(mask, (batch, 1, 1))
-    low = -1e30
-    mask = jnp.pad(mask, ((0, 0), (0, 0), (0, ROWS - CELLS)), constant_values=low)
+    shut = -1e30
+    mask = jnp.pad(mask, ((0, 0), (0, 0), (0, ROWS - CELLS)), constant_values=shut)
     mask = jnp.pad(mask, ((0, 0), (0, ROWS - CELLS), (0, 0)))
-    mask = mask.at[:, CELLS:, CELLS:].set(low)
+    mask = mask.at[:, CELLS:, CELLS:].set(shut)
     mask = mask.reshape(-1, 2, ROWS, ROWS)
-    other = jnp.full_like(mask[:, 0], low)
+    other = jnp.full_like(mask[:, 0], shut)
     mask = jnp.concatenate(
         [jnp.concatenate([mask[:, 0], other], 2), jnp.concatenate([other, mask[:, 1]], 2)], 1
     )
@@ -286,8 +539,8 @@
     bias = jnp.pad(bias, ((0, 0), (0, ROWS - CELLS), (0, ROWS - CELLS)))
     bias = jnp.tile(bias, (1, 2, 2)).reshape(heads * PAIR, PAIR)
 
-    source = pad_windows(roll_ahead(tokens.reshape(batch, tile_rows, tile_cols, dim)))
-    grad_out = pad_windows(roll_ahead(cotangent.reshape(batch, tile_rows, tile_cols, dim)))
+    source = pad_windows(join_ahead(tile, *blocks[0]))
+    grad_out = pad_windows(join_ahead(grad_tile, *blocks[1]))
     source = source.astype(F32)
 
     unit_one, scaled_one = normalize(source)
@@ -305,7 +558,7 @@
 
     def to_tile(field):
         field = field.reshape(-1, ROWS, dim)[:, :CELLS]
-        return roll_behind(from_windows(field, batch, tile_rows, tile_cols)).reshape(tokens.shape)
+        return from_windows(field, batch, tile_rows, tile_cols)
 
     output = to_tile(output)
 
@@ -338,22 +591,50 @@
     input_grad = normalize_back(grad_first, unit_one, scaled_one, gain_one) + grad_resid
     input_grad = to_tile(input_grad.astype(BF16))
 
-    sum_fc2 = reduce_rows(grad_fc2)
-    sum_fc1 = reduce_rows(grad_fc1)
-    sum_proj = reduce_rows(grad_proj)
-    sum_qkv = reduce_rows(grad_qkv)
-    count = lax.axis_size("dp")
+    def rows_of(matrix):
+        return [m.reshape(count, share, dim) for m in columns(matrix.astype(BF16))]
+
     vectors = [
         grad_gain1, grad_shift1, grad_qkvb[:dim], grad_qkvb[2 * dim :], grad_pbias, grad_gain2,
         grad_shift2, grad_fc2b, grad_fc1b,
     ]
-    joined = lax.psum(jnp.concatenate(vectors + [grad_table.reshape(-1)]), ("dp", "seq"))
+    table_row = -(-small_size // dim)
+    table_size = -(-grad_table.size // count)
+    short = jnp.concatenate([v.reshape(count, -1) for v in vectors], 1)
+    short = jnp.pad(short, ((0, 0), (0, table_row * dim - small_size)))
+    spread = jnp.pad(grad_table.reshape(-1), (0, table_size * count - grad_table.size))
+    short = jnp.concatenate([short, spread.reshape(count, -1)], 1)
+    short = jnp.pad(short, ((0, 0), (0, tail * dim - short.shape[1]))).reshape(count, tail, dim)
+    grads = jnp.concatenate(
+        rows_of(grad_qkv)
+        + rows_of(grad_proj)
+        + rows_of(grad_fc1)
+        + [grad_fc2.astype(BF16).reshape(count, -1, dim), short.astype(BF16)],
+        1,
+    )
+    edges = [edges_behind(output), edges_behind(input_grad)]
+    summed, tables, *blocks = reduce_all(grads, pack_edges(edges), low, seq_count, count)
+    blocks = unpack_edges(blocks, edges)
+    output = join_behind(output, *blocks[0]).reshape(tokens.shape)
+    input_grad = join_behind(input_grad, *blocks[1]).reshape(tokens.shape)
+    summed = summed.astype(F32)
+
+    def matrix_sum(at, blocks_wide):
+        parts = [summed[at + j * share : at + (j + 1) * share] for j in range(blocks_wide)]
+        return parts[0] if blocks_wide == 1 else jnp.concatenate(parts, 1)
+
+    sum_qkv = matrix_sum(0, 3)
+    sum_proj = matrix_sum(3 * share, 1)
+    sum_fc1 = matrix_sum(4 * share, wide)
+    sum_fc2 = summed[(4 + wide) * share : low]
+    short = summed[low:].reshape(-1)
     owned, at = [], 0
     for v in vectors:
         size = v.shape[0] // count
-        owned.append(lax.dynamic_slice(joined, (at + lax.axis_index("dp") * size,), (size,)))
-        at += v.shape[0]
-    table_total = joined[at:].reshape(bias_table.shape)
+        owned.append(short[at : at + size])
+        at += size
+    table_total = tables.astype(F32)[:, table_row:].reshape(count, -1)[:, :table_size]
+    table_total = table_total.reshape(-1)[: bias_table.size].reshape(bias_table.shape)
     s_gain1, s_shift1, s_qb, s_vb, s_pb, s_gain2, s_shift2, s_fc2b, s_fc1b = owned
     return (
         output,

time: 732 us -> 296 us (0.40)
  waiting for transfers between devices: 385 us -> 0 us
  blocking collectives: 158 us -> 0 us
  Pallas kernels: 25.8 us -> 148 us
  local copies, waits for them, and re-layouts: 48 us -> 85.4 us
  matrix products: 60.7 us -> 39.6 us
  starting transfers between devices: 15.9 us -> 0 us
  between operations: 15.6 us -> 1.9 us
    reduce_scatter x4 -> x0, waiting for transfers between devices: 360 us -> none  [reduce_rows(): lax.psum_scatter(grad.astype(BF16), ('dp', 'seq'), scatter_dimension=0, t...]
    pallas_call x0 -> x2, Pallas kernels: none -> 122 us  [the longest x1 75.1 us: reduce_all(): pl.pallas_call(functools.partial(reduce_kernel, n, nd, low), out_shape=sh...]
    all_gather x6 -> x0, blocking collectives: 118 us -> none  [the longest x1 71.2 us: gather_rows(): return lax.all_gather(mine, ('dp', 'seq'), axis=0, tiled=True)]
    psum x1 -> x0, blocking collectives: 39.2 us -> none  [local(): lax.psum(jnp.concatenate(vectors + [grad_table.reshape(-1)]), ('dp', 'seq'))]
    all_gather x3 -> x0, waiting for transfers between devices: 22.8 us -> none  [gather_rows(): return lax.all_gather(mine, ('dp', 'seq'), axis=0, tiled=True)]
    unnamed x89 -> x115, local copies, waits for them, and re-layouts: 2.96 us -> 21 us
    ppermute x12 -> x0, starting transfers between devices: 15.3 us -> none  [send(): return lax.ppermute(value, 'seq', pairs)]
    slice x17 -> x30, local copies, waits for them, and re-layouts: 6.16 us -> 18.1 us  [the longest x5 5.26 us: unpack_edges(): field.append(rows[at:at + size].reshape(b.shape))]
  transfers between devices with their start and end apart: 19 -> 0, of which waited for: 7 -> 0; matrix products, arithmetic and copies ran while one was open for 15% -> 0% of each run, Pallas kernels for 4% -> 0%
where the time goes in v2:
time: 296 us; the launch traced here: 292 us
  Pallas kernels  148 us (50%)
  local copies, waits for them, and re-layouts  85.4 us (29%)
  matrix products  39.6 us (13%)
  other arithmetic  17.2 us (6%)
    pallas_call x1, Pallas kernels, reduce_all(): pl.pallas_call(functools.partial(reduce_kernel, n, nd, low), out_shape=sh...  75.1 us
    pallas_call x1, Pallas kernels, gather_all(): pl.pallas_call(functools.partial(gather_kernel, n, nd), out_shape=shapes,...  46.8 us
    unnamed x115, local copies, waits for them, and re-layouts  21 us
    dot_general x4, matrix products, dot_nt(): lax.dot_general(left, right, (((1,), (1,)), ((), ())), preferred_element_...  15.6 us
    pallas_call x1, Pallas kernels, attend_back(): pl.pallas_call(functools.partial(attend_back_kernel, (dim // heads) ** (-...  14.8 us
    pallas_call x1, Pallas kernels, attend(): pl.pallas_call(functools.partial(attend_kernel, (dim // heads) ** (-0.5),...  11 us
    dot_general x4, matrix products, dot_tn(): lax.dot_general(left, right, (((0,), (0,)), ((), ())), preferred_element_...  10.9 us
    dot_general x4, matrix products, dot_nn(): return jnp.dot(left, right, preferred_element_type=F32)  10.8 us

profile of v2, /device:TPU:0, one launch (start us, length us, event | category | flops | bytes accessed | tf_op | source)
XLA Modules:
  0.0 291.9 jit_solution(14963135488083765615)
XLA Ops:
  0.7 6.1 %concatenate.97 = bf16[768]{0:T(1024)(128)(2,1)S(1)} concatenate(bf16[64]{0:T(256)(128)(2,1)} %param.22, bf16[64]{0:T(256)(128)(2,1)} %param.23, bf16[64]{0:T(256)(128)(2,1)} %param.25, bf16[64]{0:T(256)(128)(2,1)} %param.26, bf16[64]{0:T(256)(128)(2,1)} %param.28, bf16[64]{0:T(256)(128)(2,1)} %param.29, bf16[64]{0:T(256)(128)(2,1)} %param.30, bf16[64]{0:T(256)(128)(2,1)} %param.34, ...), dimensions={0} | concatenate | bytes 3072 | tf_op jit(solution)/shard_map/concatenate | solution.py:487
  11.6 5.1 %scatter.4 = f32[16,56,56]{2,1,0:T(8,128)S(1)} dynamic-update-slice(f32[16,56,56]{2,1,0:T(8,128)S(1)} %pad_select_fusion, f32[16,7,7]{2,1,0:T(8,128)S(1)} %broadcast.154, s32[]{:T(128)} %constant.86.clone.1, s32[]{:T(128)} %constant.94.clone.1, s32[]{:T(128)} %constant.94.clone.1) | dynamic-update-slice | bytes 6276 | tf_op jit(solution)/shard_map/scatter | solution.py:529
  27.8 1.9 tile.8
  29.8 3.8 %tile.9 = f32[1792,112]{0,1:T(8,128)} reshape(f32[16,2,56,2,56]{2,1,0,4,3:T(2,128)S(1)} %tile.8) | data formatting | bytes 1605632 | tf_op jit(solution)/shard_map/tile | solution.py:540
  33.6 2.4 copy.96.bias_ref
  36.0 46.8 %shard_map.297 = (bf16[8,832,512]{2,1,0:T(8,128)(2,1)}, bf16[160,512]{1,0:T(8,128)(2,1)}, bf16[160,512]{1,0:T(8,128)(2,1)}, bf16[32,512]{1,0:T(8,128)(2,1)}) custom-call(bf16[832,512]{1,0:T(8,128)(2,1)} %constant_dynamic-update-slice_fusion.w_ref, bf16[160,512]{1,0:T(8,128)(2,1)} %fusion.35.e0, bf16[160,512]{1,0:T(8,128)(2,1)} %fusion.36.e1, ...), custom_call_target="tpu_custom_call" | custom-call | tf_op jit(solution)/shard_map/pallas_call | solution.py:162
  82.8 1.7 fusion.58
  92.3 3.6 %slice.349 = bf16[8,256,512]{2,1,0:T(8,128)(2,1)} slice(bf16[8,832,512]{2,1,0:T(8,128)(2,1)} %get-tuple-element.44), slice={[0:8], [512:768], [0:512]} | slice | bytes 4194304 | tf_op jit(solution)/shard_map/slice | solution.py:512
  96.0 1.9 fusion.52
  100.4 3.4 %add_convert_fusion.qkv_ref = bf16[896,1536]{1,0:T(8,128)(2,1)} fusion(bf16[896,512]{1,0:T(8,128)(2,1)S(1)} %add_convert_fusion.3, f32[1536]{0:T(1024)S(1)} %pad_maximum_fusion.8, bf16[512,512]{1,0:T(8,128)(2,1)S(1)} %bitcast.140, bf16[512,512]{1,0:T(8,128)(2,1)S(1)} %bitcast.142, bf16[512,512]{1,0:T(8,128)(2,1)S(1)} %bitcast.144), kind=kOutput, calls=%fused_computation.9 | convolution fusion | flops 1416757248 | bytes 5249024 | tf_op jit(solution)/shard_map/dot_general | solution.py:331
  103.8 11.0 %shard_map.298 = (bf16[896,512]{1,0:T(8,128)(2,1)}, bf16[8,1792,112]{2,1,0:T(8,128)(2,1)}) custom-call(bf16[896,1536]{1,0:T(8,128)(2,1)} %add_convert_fusion.qkv_ref, f32[1792,112]{1,0:T(8,128)} %copy.96.bias_ref, f32[8,112,112]{2,1,0:T(8,128)} %select_maximum_fusion.mask_ref), custom_call_target="tpu_custom_call" | custom-call | flops 822083584 | bytes 3670016 | tf_op jit(solution)/shard_map/pallas_call | solution.py:383
  114.9 2.0 fusion.64
  118.9 2.4 multiply_convert_fusion
  121.3 5.0 %fusion.65 = (bf16[2048]{0:T(1024)(128)(2,1)S(1)}, bf16[896,2048]{1,0:T(8,128)(2,1)S(1)}) fusion(f32[896,2048]{1,0:T(8,128)S(1)} %get-tuple-element.187, f32[2048]{0:T(1024)S(1)} %bitcast.159, bf16[896,512]{1,0:T(8,128)(2,1)S(1)} %bitcast.116, bf16[2048,512]{1,0:T(8,128)(2,1)S(1)} %bitcast.124), kind=kOutput, calls=%fused_computation.157 | convolution fusion | flops 1901066240 | bytes 14036992 | tf_op jit(solution)/shard_map/dot_general | solution.py:323
  126.4 3.0 %add_convert_fusion.1 = bf16[896,512]{1,0:T(8,128)(2,1)} fusion(f32[896,512]{1,0:T(8,128)S(1)} %get-tuple-element.184, bf16[896,2048]{1,0:T(8,128)(2,1)S(1)} %get-tuple-element.186, bf16[2048,512]{1,0:T(8,128)(2,1)S(1)} %bitcast.125, f32[512]{0:T(512)S(1)} %reshape.539), kind=kOutput, calls=%fused_computation.32 | convolution fusion | flops 1880424448 | bytes 8521728 | tf_op jit(solution)/shard_map/dot_general | solution.py:331
  129.4 3.7 %convolution_convert_fusion = bf16[2048,512]{1,0:T(8,128)(2,1)} fusion(bf16[896,2048]{1,0:T(8,128)(2,1)S(1)} %get-tuple-element.186, bf16[896,512]{1,0:T(8,128)(2,1)S(1)} %bitcast.117), kind=kOutput, calls=%fused_computation.10 | convolution fusion | flops 1880096768 | bytes 6684672 | tf_op jit(solution)/shard_map/dot_general | solution.py:327
  133.2 3.7 %multiply_reduce_fusion = (bf16[512]{0:T(512)(128)(2,1)S(1)}, f32[896]{0:T(1024)S(1)}, f32[896]{0:T(1024)S(1)}, bf16[512]{0:T(512)(128)(2,1)S(1)}, f32[896,512]{1,0:T(8,128)}) fusion(f32[896,512]{1,0:T(8,128)S(1)} %get-tuple-element.184, f32[896]{0:T(1024)S(1)} %add_rsqrt_fusion.1, f32[896]{0:T(1024)S(1)} %broadcast_multiply_fusion.5, ...), kind=kOutput, calls=%fused_computation.33 | convolution fusion | flops 1891562752 | bytes 9455616 | tf_op jit(solution)/shard_map/dot_general | solution.py:323
  136.8 2.6 reshape.541
  139.4 2.5 copy.120
  142.1 2.6 fusion.51
  145.8 2.7 convolution_convert_fusion.1
  148.5 1.5 convolution_convert_fusion.5
  150.0 1.4 fusion.53
  156.2 3.1 %convolution_convert_fusion.4.do_ref = bf16[896,512]{1,0:T(8,128)(2,1)} fusion(bf16[512,512]{1,0:T(8,128)(2,1)S(1)} %bitcast.114, f32[896,512]{1,0:T(8,128)} %copy-done.2), kind=kOutput, calls=%fused_computation.44 | convolution fusion | flops 470679552 | bytes 3276800 | tf_op jit(solution)/shard_map/dot_general | solution.py:323
  159.3 14.8 %shard_map.299 = (bf16[896,1536]{1,0:T(8,128)(2,1)}, f32[1792,112]{1,0:T(8,128)}) custom-call(bf16[896,1536]{1,0:T(8,128)(2,1)} %add_convert_fusion.qkv_ref, bf16[896,512]{1,0:T(8,128)(2,1)} %convolution_convert_fusion.4.do_ref, bf16[8,1792,112]{2,1,0:T(8,128)(2,1)} %get-tuple-element.46.p_ref), custom_call_target="tpu_custom_call" | custom-call | flops 1644167168 | bytes 7340032 | tf_op jit(solution)/shard_map/pallas_call | solution.py:410
  174.2 3.8 %fusion.15 = (f32[896]{0:T(1024)S(1)}, bf16[512]{0:T(512)(128)(2,1)S(1)}, f32[896]{0:T(1024)S(1)}, bf16[896,512]{1,0:T(8,128)(2,1)S(1)}) fusion(f32[16,56,512]{2,1,0:T(8,128)S(1)} %copy.86, f32[512]{0:T(512)S(1)} %reshape.531, f32[896]{0:T(1024)S(1)} %rsqrt.20, f32[896]{0:T(1024)S(1)} %div.35, bf16[896,1536]{1,0:T(8,128)(2,1)} %get-tuple-element.47, ...), kind=kOutput, calls=%fused_computation.26 | convolution fusion | flops 1418589952 | bytes 7095296 | tf_op jit(solution)/shard_map/dot_general | solution.py:323
  179.7 2.8 fusion.14
  182.5 2.5 reshape.542
  185.0 2.5 copy.119
  187.9 3.0 %convolution_convert_fusion.2 = bf16[512,1536]{1,0:T(8,128)(2,1)S(1)} fusion(bf16[896,512]{1,0:T(8,128)(2,1)} %copy-done.10, bf16[896,1536]{1,0:T(8,128)(2,1)S(1)} %copy-done.5), kind=kOutput, calls=%fused_computation.12 | convolution fusion | flops 1410072576 | bytes 5242880 | tf_op jit(solution)/shard_map/dot_general | solution.py:327
  201.2 2.8 copy-done.6
  204.0 75.1 %shard_map.300 = (bf16[832,512]{1,0:T(8,128)(2,1)}, bf16[8,16,512]{2,1,0:T(8,128)(2,1)}, bf16[160,512]{1,0:T(8,128)(2,1)}, bf16[160,512]{1,0:T(8,128)(2,1)}, bf16[32,512]{1,0:T(8,128)(2,1)}) custom-call(bf16[8,832,512]{2,1,0:T(8,128)(2,1)} %copy-done.6, bf16[160,512]{1,0:T(8,128)(2,1)} %fusion.37.e0, bf16[160,512]{1,0:T(8,128)(2,1)} %fusion.38.e1, ...), custom_call_target="tpu_custom_call" | custom-call | tf_op jit(solution)/shard_map/pallas_call | solution.py:262
  (263 shorter events, 58.6 us)
Async XLA Ops:
  0.6 8.1 %copy-start = (f32[169,16]{0,1:T(8,128)S(1)}, f32[169,16]{0,1:T(8,128)}, u32[]{:S(2)}) copy-start(f32[169,16]{0,1:T(8,128)} %param.35) | copy-start | bytes 32452
  11.3 6.4 %copy-start.40 = (bf16[64,1536]{1,0:T(8,128)(2,1)S(1)}, bf16[64,1536]{1,0:T(8,128)(2,1)}, u32[]{:S(2)}) copy-start(bf16[64,1536]{1,0:T(8,128)(2,1)} %param.24) | copy-start | bytes 589828
  11.3 8.3 %copy-start.41 = (bf16[64,512]{1,0:T(8,128)(2,1)S(1)}, bf16[64,512]{1,0:T(8,128)(2,1)}, u32[]{:S(2)}) copy-start(bf16[64,512]{1,0:T(8,128)(2,1)} %param.27) | copy-start | bytes 196612
  11.5 8.7 %copy-start.38 = (bf16[64,2048]{1,0:T(8,128)(2,1)S(1)}, bf16[64,2048]{1,0:T(8,128)(2,1)}, u32[]{:S(2)}) copy-start(bf16[64,2048]{1,0:T(8,128)(2,1)} %param.31) | copy-start | bytes 786436
  11.5 11.2 %copy-start.39 = (bf16[256,512]{1,0:T(8,128)(2,1)S(1)}, bf16[256,512]{1,0:T(8,128)(2,1)}, u32[]{:S(2)}) copy-start(bf16[256,512]{1,0:T(8,128)(2,1)} %param.33) | copy-start | bytes 786436
  11.6 12.4 %copy-start.24 = (bf16[1,1,784,512]{3,2,1,0:T(8,128)(2,1)S(1)}, bf16[1,1,784,512]{3,2,1,0:T(8,128)(2,1)}, u32[]{:S(2)}) copy-start(bf16[1,1,784,512]{3,2,1,0:T(8,128)(2,1)} %param.20) | copy-start | bytes 2408452
  90.9 5.0 %slice-start = ((s8[6815744]{0:T(1024)(128)(4,1)}), s8[4194304]{0:T(1024)(128)(4,1)S(1)}, s32[]{:S(2)}) async-start(s8[6815744]{0:T(1024)(128)(4,1)} %bitcast.111), calls=%async_computation | async-start | bytes 8388608
  91.3 4.7 %slice-start.1 = ((s8[6815744]{0:T(1024)(128)(4,1)}), s8[2621440]{0:T(1024)(128)(4,1)S(1)}, s32[]{:S(2)}) async-start(s8[6815744]{0:T(1024)(128)(4,1)} %bitcast.111), calls=%async_computation.1 | async-start | bytes 5242880
  98.9 1.6 copy-start.30
  114.9 2.4 copy-start.35
  116.8 16.3 %copy-start.3 = (f32[896,512]{1,0:T(8,128)}, f32[896,512]{1,0:T(8,128)S(1)}, u32[]{:S(2)}) copy-start(f32[896,512]{1,0:T(8,128)S(1)} %get-tuple-element.184) | copy-start | bytes 5505028
  116.9 1.9 copy-start.33
  116.9 2.0 copy-start.34
  118.9 2.4 copy-start.17
  126.4 6.8 %copy-start.8 = (bf16[896,2048]{1,0:T(8,128)(2,1)}, bf16[896,2048]{1,0:T(8,128)(2,1)S(1)}, u32[]{:S(2)}) copy-start(bf16[896,2048]{1,0:T(8,128)(2,1)S(1)} %get-tuple-element.190) | copy-start | bytes 11010052
  142.1 2.6 copy-start.4
  142.1 3.7 %copy-start.9 = (bf16[896,2048]{1,0:T(8,128)(2,1)S(1)}, bf16[896,2048]{1,0:T(8,128)(2,1)}, u32[]{:S(2)}) copy-start(bf16[896,2048]{1,0:T(8,128)(2,1)} %copy-done.8) | copy-start | bytes 11010052
  145.8 2.7 copy-start.2
  145.8 2.7 copy-start.11
  150.0 1.6 copy-start.14
  159.3 14.8 %copy-start.27 = (bf16[8,64,512]{2,1,0:T(8,128)(2,1)S(1)}, bf16[8,64,512]{2,1,0:T(8,128)(2,1)}, u32[]{:S(2)}) copy-start(bf16[8,64,512]{2,1,0:T(8,128)(2,1)} %get-tuple-element.132) | copy-start | bytes 1572868
  159.3 14.8 %copy-start.29 = (bf16[8,64,512]{2,1,0:T(8,128)(2,1)S(1)}, bf16[8,64,512]{2,1,0:T(8,128)(2,1)}, u32[]{:S(2)}) copy-start(bf16[8,64,512]{2,1,0:T(8,128)(2,1)} %get-tuple-element.133) | copy-start | bytes 1572868
  159.3 14.9 %copy-start.31 = (bf16[8,64,512]{2,1,0:T(8,128)(2,1)S(1)}, bf16[8,64,512]{2,1,0:T(8,128)(2,1)}, u32[]{:S(2)}) copy-start(bf16[8,64,512]{2,1,0:T(8,128)(2,1)} %get-tuple-element.134) | copy-start | bytes 1572868
  174.2 3.8 %copy-start.23 = (f32[1792,112]{1,0:T(8,128)S(1)}, f32[1792,112]{1,0:T(8,128)}, u32[]{:S(2)}) copy-start(f32[1792,112]{1,0:T(8,128)} %get-tuple-element.48) | copy-start | bytes 2408452
  182.5 5.0 %copy-start.5 = (bf16[896,1536]{1,0:T(8,128)(2,1)S(1)}, bf16[896,1536]{1,0:T(8,128)(2,1)}, u32[]{:S(2)}) copy-start(bf16[896,1536]{1,0:T(8,128)(2,1)} %get-tuple-element.47) | copy-start | bytes 8257540
  190.9 1.7 copy-start.13
  195.0 3.0 %copy-start.18 = (bf16[512,512]{1,0:T(8,128)(2,1)S(1)}, bf16[512,512]{1,0:T(8,128)(2,1)}, u32[]{:S(2)}) copy-start(bf16[512,512]{1,0:T(8,128)(2,1)} %get-tuple-element.140) | copy-start | bytes 1572868
  195.7 2.4 copy-start.15
  199.1 1.7 copy-start.16
  201.2 2.8 copy-start.6
  283.9 1.6 copy-start.12
  288.6 3.1 %copy-start.1 = (f32[169,16]{0,1:T(8,128)S(1)}, f32[169,16]{0,1:T(8,128)}, u32[]{:S(2)}) copy-start(f32[169,16]{0,1:T(8,128)} %param.35) | copy-start | bytes 32452
  (12 other events, 14.7 us)
